TPU v7x, 32 devices: a whole 2x2x4 slice. The times are simulated.
32 devices in a mesh: parts: 2 (over x), blk: 8 (over z, y), section: 2 (over core).
Axes of the slice: x: 2, y: 2, z: 4, core: 2. Of those that a mesh axis runs over, the one named last changes fastest.
Arguments:
- points: float32 [8, 16384], P(None, ('parts', 'blk')), parts along dimension 1, may hold values from -6 to 6
- rhs: float32 [8, 16384], P(None, ('parts', 'blk')), parts along dimension 1, may hold values from -6 to 6
- scales: float32 [16], P('parts'), parts along dimension 0, may hold values from 1 to 4
Outputs:
- product: float32 [8, 16384], P(None, ('parts', 'blk')), parts along dimension 1
There are 2 independent parts, one for each index of `parts`. A program takes and returns all parts, laid end to end along the dimension named above; each array names one. Nothing has to cross between parts.
All inputs are finite; a program needn't handle non-finite values.
Results may differ from a plain program's by a relative error of at most 0.00009.
Values sent between devices are 32-bit elements; how exact they have to be, the bound alone decides.
No kernel may reach another device: no remote copies, remote signals or barrier semaphores. Data moves between devices by JAX's collectives and lax.ppermute only.
A program may use at most 64 MiB of HBM per device.

v0:
```python
import math

import jax
import jax.numpy as jnp
from jax import lax
from jax.sharding import PartitionSpec as P

ROOT5 = math.sqrt(5.0)
NOISE = 0.1


def matern(row_points, col_points):
    row_norms = jnp.sum(row_points * row_points, axis=0)
    col_norms = jnp.sum(col_points * col_points, axis=0)
    products = lax.dot_general(
        row_points,
        col_points,
        (((0,), (0,)), ((), ())),
        precision=lax.Precision.HIGHEST,
        preferred_element_type=jnp.float32,
    )
    squared = jnp.maximum(row_norms[:, None] + col_norms[None, :] - 2.0 * products, 0.0)
    distance = jnp.sqrt(squared)
    return (1.0 + ROOT5 * distance + 5.0 / 3.0 * squared) * jnp.exp(-ROOT5 * distance)


def apply_right(values, kernel_tile):
    return lax.dot_general(
        values,
        kernel_tile,
        (((1,), (1,)), ((), ())),
        precision=lax.Precision.HIGHEST,
        preferred_element_type=jnp.float32,
    )


def partner_of(round_index, own_index, block_count):
    modulus = block_count - 1
    others = (round_index - own_index) % modulus
    lonely = (2 * own_index - round_index) % modulus == 0
    others = jnp.where(lonely, modulus, others)
    last_partner = round_index * (block_count // 2) % modulus
    return jnp.where(own_index == modulus, last_partner, others)


def local(points, rhs, scales):
    block_count = lax.axis_size("blk")
    own_index = lax.axis_index("blk")
    section_index = lax.axis_index("section")
    block_width = points.shape[1]
    round_count = block_count - 1
    scaled = points / scales[:, None]
    all_points, all_values = (
        lax.all_gather(scaled, "blk", axis=1, tiled=True),
        lax.all_gather(rhs, "blk", axis=1, tiled=True),
    )

    def advance(counter, partial_value):
        round_index = 2 * counter + section_index
        partner = jnp.where(
            round_index < round_count,
            partner_of(jnp.minimum(round_index, round_count - 1), own_index, block_count),
            own_index,
        )
        col_points = lax.dynamic_slice_in_dim(all_points, partner * block_width, block_width, 1)
        col_values = lax.dynamic_slice_in_dim(all_values, partner * block_width, block_width, 1)
        kernel_tile = matern(scaled, col_points)
        return partial_value + apply_right(col_values, kernel_tile)

    partial_value = lax.fori_loop(0, block_count // 2, advance, jnp.zeros(rhs.shape, jnp.float32))
    summed = lax.psum(partial_value, "section")
    return summed + NOISE * rhs


def solution(mesh):
    in_specs = (P(None, ("parts", "blk")), P(None, ("parts", "blk")), P("parts"))
    out_specs = P(None, ("parts", "blk"))
    return jax.shard_map(local, mesh=mesh, in_specs=in_specs, out_specs=out_specs, check_vma=False)
```

profile of v0, /device:TPU:0, one launch (start us, length us, event | category | flops | bytes accessed | tf_op | source)
XLA Modules:
  0.0 101.4 jit_solution(5462143429454454726)
XLA Ops:
  0.0 0.8 multiply_reduce_fusion.1
  0.9 32.5 %all_gather.7 = f32[8,8192]{1,0:T(8,128)S(1)} all-gather(f32[8,1024]{1,0:T(8,128)S(1)} %get-tuple-element.326), channel_id=1, replica_groups=mesh['parts'=2,'blk'=8,'section'=2] {'blk'}, dimensions={1}, use_global_device_ids=true | all-gather | bytes 294912 | tf_op jit(solution)/shard_map/all_gather | solution.py:54
  33.4 30.9 %all_gather.6 = f32[8,8192]{1,0:T(8,128)S(1)} all-gather(f32[8,1024]{1,0:T(8,128)} %param.6), channel_id=1, replica_groups=mesh['parts'=2,'blk'=8,'section'=2] {'blk'}, dimensions={1}, use_global_device_ids=true | all-gather | bytes 294912 | tf_op jit(solution)/shard_map/all_gather | solution.py:55
  64.3 0.0 copy-start
  64.3 33.0 %while.16 = (s32[]{:T(128)}, f32[8,1024]{1,0:T(8,128)S(1)}, s32[]{:T(128)}, s32[]{:T(128)}, s32[]{:T(128)}, /*index=5*/pred[]{:T(512)}, f32[8,8192]{1,0:T(8,128)...) while((s32[]{:T(128)}, f32[8,1024]{1,0:T(8,128)S(1)}, ...), condition=%wide.region_3.4_spmd.clone, body=%wide.region_1.3_spmd.clone.sunk | while | flops 211844128 | bytes 8598048 | solution.py:70
  64.4 3.5 %fusion.46 = f32[1024,1024]{1,0:T(8,128)S(1)} fusion(f32[8,1024]{1,0:T(8,128)S(1)} %get-tuple-element.362, f32[8,8192]{1,0:T(8,128)S(1)} %get-tuple-element.361, s32[]{:T(128)S(6)} %select_n.104), kind=kOutput, calls=%fused_computation.24.clone.1 | convolution fusion | flops 100663296 | bytes 4259844 | tf_op jit(solution)/shard_map/while/body/eval_jaxpr/dot_general | solution.py:15
  67.9 4.7 %fusion.47 = f32[8,1024]{1,0:T(8,128)S(1)} fusion(f32[1024,1024]{1,0:T(8,128)S(1)} %fusion.46, f32[1024]{0:T(1024)S(1)} %multiply_reduce_fusion.3, f32[1024]{0:T(1024)S(1)} %get-tuple-element.360, f32[8,1024]{1,0:T(8,128)S(1)} %get-tuple-element.336, f32[8,8192]{1,0:T(8,128)S(1)} %get-tuple-element.359, s32[]{:T(128)S(6)} %select_n.104, pred[]{:T(512)S(6)} %compare.3), kind=kOutput, calls=%fused_computation.21.clone.1 | convolution fusion | flops 111165440 | bytes 4300805 | tf_op jit(solution)/shard_map/while/body/eval_jaxpr/dot_general | solution.py:28
  72.6 3.5 %fusion.46 = f32[1024,1024]{1,0:T(8,128)S(1)} fusion(f32[8,1024]{1,0:T(8,128)S(1)} %get-tuple-element.362, f32[8,8192]{1,0:T(8,128)S(1)} %get-tuple-element.361, s32[]{:T(128)S(6)} %select_n.104), kind=kOutput, calls=%fused_computation.24.clone.1 | convolution fusion | flops 100663296 | bytes 4259844 | tf_op jit(solution)/shard_map/while/body/eval_jaxpr/dot_general | solution.py:15
  76.2 4.7 %fusion.47 = f32[8,1024]{1,0:T(8,128)S(1)} fusion(f32[1024,1024]{1,0:T(8,128)S(1)} %fusion.46, f32[1024]{0:T(1024)S(1)} %multiply_reduce_fusion.3, f32[1024]{0:T(1024)S(1)} %get-tuple-element.360, f32[8,1024]{1,0:T(8,128)S(1)} %get-tuple-element.336, f32[8,8192]{1,0:T(8,128)S(1)} %get-tuple-element.359, s32[]{:T(128)S(6)} %select_n.104, pred[]{:T(512)S(6)} %compare.3), kind=kOutput, calls=%fused_computation.21.clone.1 | convolution fusion | flops 111165440 | bytes 4300805 | tf_op jit(solution)/shard_map/while/body/eval_jaxpr/dot_general | solution.py:28
  80.9 3.5 %fusion.46 = f32[1024,1024]{1,0:T(8,128)S(1)} fusion(f32[8,1024]{1,0:T(8,128)S(1)} %get-tuple-element.362, f32[8,8192]{1,0:T(8,128)S(1)} %get-tuple-element.361, s32[]{:T(128)S(6)} %select_n.104), kind=kOutput, calls=%fused_computation.24.clone.1 | convolution fusion | flops 100663296 | bytes 4259844 | tf_op jit(solution)/shard_map/while/body/eval_jaxpr/dot_general | solution.py:15
  84.4 4.7 %fusion.47 = f32[8,1024]{1,0:T(8,128)S(1)} fusion(f32[1024,1024]{1,0:T(8,128)S(1)} %fusion.46, f32[1024]{0:T(1024)S(1)} %multiply_reduce_fusion.3, f32[1024]{0:T(1024)S(1)} %get-tuple-element.360, f32[8,1024]{1,0:T(8,128)S(1)} %get-tuple-element.336, f32[8,8192]{1,0:T(8,128)S(1)} %get-tuple-element.359, s32[]{:T(128)S(6)} %select_n.104, pred[]{:T(512)S(6)} %compare.3), kind=kOutput, calls=%fused_computation.21.clone.1 | convolution fusion | flops 111165440 | bytes 4300805 | tf_op jit(solution)/shard_map/while/body/eval_jaxpr/dot_general | solution.py:28
  89.1 3.5 %fusion.46 = f32[1024,1024]{1,0:T(8,128)S(1)} fusion(f32[8,1024]{1,0:T(8,128)S(1)} %get-tuple-element.362, f32[8,8192]{1,0:T(8,128)S(1)} %get-tuple-element.361, s32[]{:T(128)S(6)} %select_n.104), kind=kOutput, calls=%fused_computation.24.clone.1 | convolution fusion | flops 100663296 | bytes 4259844 | tf_op jit(solution)/shard_map/while/body/eval_jaxpr/dot_general | solution.py:15
  92.7 4.7 %fusion.47 = f32[8,1024]{1,0:T(8,128)S(1)} fusion(f32[1024,1024]{1,0:T(8,128)S(1)} %fusion.46, f32[1024]{0:T(1024)S(1)} %multiply_reduce_fusion.3, f32[1024]{0:T(1024)S(1)} %get-tuple-element.360, f32[8,1024]{1,0:T(8,128)S(1)} %get-tuple-element.336, f32[8,8192]{1,0:T(8,128)S(1)} %get-tuple-element.359, s32[]{:T(128)S(6)} %select_n.104, pred[]{:T(512)S(6)} %compare.3), kind=kOutput, calls=%fused_computation.21.clone.1 | convolution fusion | flops 111165440 | bytes 4300805 | tf_op jit(solution)/shard_map/while/body/eval_jaxpr/dot_general | solution.py:28
  97.3 3.4 %psum.7 = f32[8,1024]{1,0:T(8,128)S(1)} all-reduce(f32[8,1024]{1,0:T(8,128)S(1)} %get-tuple-element.200), channel_id=1, replica_groups=mesh['parts'=2,'blk'=8,'section'=2] {'section'}, use_global_device_ids=true, to_apply=%region_4.5 | all-reduce | flops 8192 | bytes 65536 | tf_op jit(solution)/shard_map/psum | solution.py:71
  100.8 0.0 copy-done
  100.8 0.6 multiply_add_fusion
  (5 shorter events, 0.1 us)
Async XLA Ops:
  64.3 36.4 %copy-start = (f32[8,1024]{1,0:T(8,128)S(1)}, f32[8,1024]{1,0:T(8,128)}, u32[]{:S(2)}) copy-start(f32[8,1024]{1,0:T(8,128)} %param.6) | copy-start | bytes 98308
where the time goes:
time: 102 us; the launch traced here: 101 us
  blocking collectives  66.9 us (66%)
  matrix products  32.9 us (32%)
  other arithmetic  1.54 us (2%)
    all_gather x1, blocking collectives, local(): lax.all_gather(scaled, 'blk', axis=1, tiled=True)  32.5 us
    all_gather x1, blocking collectives, local(): lax.all_gather(rhs, 'blk', axis=1, tiled=True)  30.9 us
    dot_general x4, matrix products, apply_right(): lax.dot_general(values, kernel_tile, (((1,), (1,)), ((), ())), precision=...  18.7 us
    dot_general x4, matrix products, matern(): lax.dot_general(row_points, col_points, (((0,), (0,)), ((), ())), precisi...  14.1 us
    psum x1, blocking collectives, local(): summed = lax.psum(partial_value, 'section')  3.4 us

commit v1 on v0

v1 whole, which is shorter than its diff:
```python
import math

import jax
import jax.numpy as jnp
from jax import lax
from jax.experimental import pallas as pl
from jax.experimental.pallas import tpu as pltpu
from jax.sharding import PartitionSpec as P

NOISE = 0.1
LOG2E = math.log2(math.e)
LN2 = math.log(2.0)
POINT_FACTOR = math.sqrt(5.0) * LOG2E
RHS_FACTOR = LN2 * LN2 / 3.0
SHIFT = 1.5 * LOG2E
REST = 0.75 * LOG2E * LOG2E
STEP = 256
DEPTH = 64


def three_parts(values):
    high = values.astype(jnp.bfloat16).astype(jnp.float32)
    rest = values - high
    middle = rest.astype(jnp.bfloat16).astype(jnp.float32)
    return high, middle, rest - middle


def factors(points, left):
    norms = jnp.sum(points * points, axis=0, keepdims=True)
    high, middle, low = three_parts(-2.0 * points if left else points)
    ones = [jnp.ones_like(norms)] * 3
    rows = [*three_parts(norms), *ones] if left else [*ones, *three_parts(norms)]
    rows.append(jnp.zeros((DEPTH - 54, points.shape[1]), jnp.float32))
    order = [high, high, middle, high, low, middle] if left else [high, middle, high, low, high, middle]
    return jnp.concatenate(order + rows, axis=0)


def multiply(a, b):
    return lax.dot_general(a, b, (((1,), (0,)), ((), ())), preferred_element_type=jnp.float32)


def tile_kernel(own_ref, other_ref, before_ref, out_ref, left_ref, total_ref):
    width = own_ref.shape[1]
    depth = other_ref.shape[1]
    right = factors(own_ref[:8], False).astype(jnp.bfloat16)
    left_ref[...] = factors(other_ref[:8], True).T.astype(jnp.bfloat16)
    values = other_ref[8:]
    high = values.astype(jnp.bfloat16).astype(jnp.float32)
    both = jnp.concatenate([high, values - high], axis=0).astype(jnp.bfloat16)
    single = jnp.concatenate([high, jnp.zeros_like(high)], axis=0).astype(jnp.bfloat16)
    total_ref[...] = jnp.zeros_like(total_ref)
    for j in range(0, depth, STEP):
        for i in range(0, width, STEP):
            squared = jnp.maximum(multiply(left_ref[j : j + STEP], right[:, i : i + STEP]), 1e-30)
            scaled = squared * lax.rsqrt(squared)
            shifted = scaled + SHIFT
            entries = (shifted * shifted + REST) * jnp.exp2(-scaled)
            rounded = entries.astype(jnp.bfloat16)
            remainder = (entries - rounded.astype(jnp.float32)).astype(jnp.bfloat16)
            total_ref[:, i : i + STEP] += multiply(both[:, j : j + STEP], rounded) + multiply(
                single[:, j : j + STEP], remainder
            )
    out_ref[...] = before_ref[...] + total_ref[:8] + total_ref[8:]


def tile(own, other, before):
    width, depth = own.shape[1], other.shape[1]
    in_vmem = pl.BlockSpec(memory_space=pltpu.VMEM)
    return pl.pallas_call(
        tile_kernel,
        out_shape=jax.ShapeDtypeStruct((8, width), jnp.float32),
        in_specs=[in_vmem] * 3,
        out_specs=in_vmem,
        scratch_shapes=[pltpu.VMEM((depth, DEPTH), jnp.bfloat16), pltpu.VMEM((16, width), jnp.float32)],
        compiler_params=pltpu.CompilerParams(vmem_limit_bytes=24 * 1024 * 1024),
        cost_estimate=pl.CostEstimate(
            flops=2 * 80 * width * depth, bytes_accessed=4 * 32 * depth, transcendentals=2 * width * depth
        ),
    )(own, other, before)


def local(points, rhs, scales):
    block_count = lax.axis_size("blk")
    section = lax.axis_index("section")
    half = block_count // 2
    mine = jnp.concatenate([points * (POINT_FACTOR / scales)[:, None], rhs * RHS_FACTOR], axis=0)
    others = []
    for step in range(half):
        pairs = [(2 * i + 1, 2 * (i ^ (half + step)) + 1) for i in range(block_count)]
        if step:
            pairs += [(2 * i, 2 * (i ^ step)) for i in range(block_count)]
        others.append(lax.ppermute(mine, ("blk", "section"), pairs))
    others[0] = jnp.where(section == 0, mine, others[0])
    total = jnp.zeros_like(rhs)
    for other in others:
        total = tile(mine, other, total)
    swapped = lax.ppermute(total, "section", [(0, 1), (1, 0)])
    return total + swapped + NOISE * rhs


def solution(mesh):
    in_specs = (P(None, ("parts", "blk")), P(None, ("parts", "blk")), P("parts"))
    out_specs = P(None, ("parts", "blk"))
    return jax.shard_map(local, mesh=mesh, in_specs=in_specs, out_specs=out_specs, check_vma=False)
```

time: 102 us -> 22.4 us (0.22)
  blocking collectives: 66.9 us -> 0 us
  matrix products: 32.9 us -> 0 us
  starting transfers between devices: 0 us -> 9.92 us
  Pallas kernels: 0 us -> 9.21 us
    all_gather x2 -> x0, blocking collectives: 63.5 us -> none  [the longest x1 32.5 us: local(): lax.all_gather(scaled, 'blk', axis=1, tiled=True)]
    dot_general x8 -> x0, matrix products: 32.9 us -> none  [the longest x4 18.7 us: apply_right(): lax.dot_general(values, kernel_tile, (((1,), (1,)), ((), ())), precision=...]
    ppermute x0 -> x5, starting transfers between devices: none -> 9.92 us  [the longest x4 5.28 us: local(): others.append(lax.ppermute(mine, ('blk', 'section'), pairs))]
    pallas_call x0 -> x4, Pallas kernels: none -> 9.21 us  [tile(): pl.pallas_call(tile_kernel, out_shape=jax.ShapeDtypeStruct((8, width), jn...]
    psum x1 -> x0, blocking collectives: 3.4 us -> none  [local(): summed = lax.psum(partial_value, 'section')]
  transfers between devices with their start and end apart: 0 -> 5, of which waited for: 0 -> 1; matrix products, arithmetic and copies ran while one was open for 0% -> 0% of each run, Pallas kernels for 0% -> 31%
where the time goes in v1:
time: 22.4 us; the launch traced here: 22.2 us
  starting transfers between devices  9.92 us (44%)
  Pallas kernels  9.21 us (41%)
  other arithmetic  2.15 us (10%)
  waiting for transfers between devices  0.87 us (4%)
    pallas_call x4, Pallas kernels, tile(): pl.pallas_call(tile_kernel, out_shape=jax.ShapeDtypeStruct((8, width), jn...  9.21 us
    ppermute x4, starting transfers between devices, local(): others.append(lax.ppermute(mine, ('blk', 'section'), pairs))  5.28 us
    ppermute x1, starting transfers between devices, local(): swapped = lax.ppermute(total, 'section', [(0, 1), (1, 0)])  4.64 us
    ppermute x1, waiting for transfers between devices, local(): swapped = lax.ppermute(total, 'section', [(0, 1), (1, 0)])  0.86 us
    mul x1, other arithmetic, local(): rhs * RHS_FACTOR  0.85 us
    div x1, other arithmetic, local(): POINT_FACTOR / scales  0.66 us
    add x1, other arithmetic, local(): return total + swapped + NOISE * rhs  0.62 us
  transfers between devices with their start and end apart: 5, of which 1 were waited for; matrix products, arithmetic and copies ran while one was open for 0% of the time, Pallas kernels for 31%

profile of v1, /device:TPU:0, one launch (start us, length us, event | category | flops | bytes accessed | tf_op | source)
XLA Modules:
  0.0 22.2 jit_solution(16058972503548490644)
XLA Ops:
  0.0 0.7 %broadcast_divide_fusion = f32[8]{0:T(128)S(1)} fusion(f32[8]{0:T(128)} %param.5), kind=kLoop, calls=%fused_computation.5 | loop fusion | flops 8 | bytes 64 | tf_op jit(solution)/shard_map/div | solution.py:86
  0.7 0.9 %broadcast_multiply_fusion = (f32[8,1024]{1,0:T(8,128)S(1)}, f32[8,1024]{1,0:T(8,128)S(1)}) fusion(f32[8,1024]{1,0:T(8,128)} %param.4, f32[8,1024]{1,0:T(8,128)} %param.3, f32[8]{0:T(128)S(1)} %broadcast_divide_fusion), kind=kLoop, calls=%fused_computation.3 | loop fusion | flops 16384 | bytes 131104 | tf_op jit(solution)/shard_map/mul | solution.py:86
  1.5 0.7 %collective-permute-start.3 = (f32[16,1024]{1,0:T(8,128)S(1)}, f32[16,1024]{1,0:T(8,128)S(1)}, u32[]{:S(2)}, u32[]{:S(2)}) collective-permute-start(f32[16,1024]{1,0:T(8,128)S(1)} %pad_maximum_fusion.own_ref), channel_id=1, source_target_pairs={{1,9},{3,11},{5,13},{7,15},{9,1},{11,3},{13,5},{15,7},{17,25},{19,... | collective-permute-start | bytes 196616 | tf_op jit(solution)/shard_map/ppermute | solution.py:92
  2.2 3.0 %collective-permute-start.2 = (f32[16,1024]{1,0:T(8,128)S(1)}, f32[16,1024]{1,0:T(8,128)S(1)}, u32[]{:S(2)}, u32[]{:S(2)}) collective-permute-start(f32[16,1024]{1,0:T(8,128)S(1)} %pad_maximum_fusion.own_ref), channel_id=1, source_target_pairs={{1,11},{3,9},{5,15},{7,13},{9,3},{11,1},{13,7},{15,5},{0,2},{2,0},... | collective-permute-start | bytes 196616 | tf_op jit(solution)/shard_map/ppermute | solution.py:92
  5.2 1.6 %collective-permute-start.1 = (f32[16,1024]{1,0:T(8,128)S(1)}, f32[16,1024]{1,0:T(8,128)S(1)}, u32[]{:S(2)}, u32[]{:S(2)}) collective-permute-start(f32[16,1024]{1,0:T(8,128)S(1)} %pad_maximum_fusion.own_ref), channel_id=1, source_target_pairs={{1,13},{3,15},{5,9},{7,11},{9,5},{11,7},{13,1},{15,3},{0,4},{2,6},... | collective-permute-start | bytes 196616 | tf_op jit(solution)/shard_map/ppermute | solution.py:92
  6.8 0.0 collective-permute-start
  6.8 0.0 collective-permute-done.3
  6.8 2.3 %shard_map.37.before_ref = f32[8,1024]{1,0:T(8,128)S(1)} custom-call(f32[16,1024]{1,0:T(8,128)S(1)} %pad_maximum_fusion.own_ref, f32[16,1024]{1,0:T(8,128)S(1)} %broadcast_select_fusion.other_ref, f32[8,1024]{1,0:T(8,128)S(1)} %broadcast_in_dim.4.before_ref), custom_call_target="tpu_custom_call" | custom-call | flops 167772160 | bytes 131072 | tf_op jit(solution)/shard_map/pallas_call | solution.py:69
  9.1 0.0 collective-permute-done.2.other_ref
  9.1 2.3 %shard_map.38.before_ref = f32[8,1024]{1,0:T(8,128)S(1)} custom-call(f32[16,1024]{1,0:T(8,128)S(1)} %pad_maximum_fusion.own_ref, f32[16,1024]{1,0:T(8,128)S(1)} %collective-permute-done.2.other_ref, f32[8,1024]{1,0:T(8,128)S(1)} %shard_map.37.before_ref), custom_call_target="tpu_custom_call" | custom-call | flops 167772160 | bytes 131072 | tf_op jit(solution)/shard_map/pallas_call | solution.py:69
  11.4 0.0 collective-permute-done.1.other_ref
  11.4 2.3 %shard_map.39.before_ref = f32[8,1024]{1,0:T(8,128)S(1)} custom-call(f32[16,1024]{1,0:T(8,128)S(1)} %pad_maximum_fusion.own_ref, f32[16,1024]{1,0:T(8,128)S(1)} %collective-permute-done.1.other_ref, f32[8,1024]{1,0:T(8,128)S(1)} %shard_map.38.before_ref), custom_call_target="tpu_custom_call" | custom-call | flops 167772160 | bytes 131072 | tf_op jit(solution)/shard_map/pallas_call | solution.py:69
  13.7 0.0 copy-start
  13.7 0.0 collective-permute-done.other_ref
  13.7 2.3 %shard_map.40 = f32[8,1024]{1,0:T(8,128)S(1)} custom-call(f32[16,1024]{1,0:T(8,128)S(1)} %pad_maximum_fusion.own_ref, f32[16,1024]{1,0:T(8,128)S(1)} %collective-permute-done.other_ref, f32[8,1024]{1,0:T(8,128)S(1)} %shard_map.39.before_ref), custom_call_target="tpu_custom_call" | custom-call | flops 167772160 | bytes 131072 | tf_op jit(solution)/shard_map/pallas_call | solution.py:69
  16.1 4.6 %collective-permute-start.4 = (f32[8,1024]{1,0:T(8,128)S(1)}, f32[8,1024]{1,0:T(8,128)S(1)}, u32[]{:S(2)}, u32[]{:S(2)}) collective-permute-start(f32[8,1024]{1,0:T(8,128)S(1)} %shard_map.40), channel_id=1, source_target_pairs={{0,1},{1,0},{2,3},{3,2},{4,5},{5,4},{6,7},{7,6},{8,9},{9,8},{10,11... | collective-permute-start | bytes 98312 | tf_op jit(solution)/shard_map/ppermute | solution.py:97
  20.7 0.9 %collective-permute-done.4 = f32[8,1024]{1,0:T(8,128)S(1)} collective-permute-done((f32[8,1024]{1,0:T(8,128)S(1)}, f32[8,1024]{1,0:T(8,128)S(1)}, u32[]{:S(2)}, u32[]{:S(2)}) %collective-permute-start.4) | collective-permute-done | bytes 32800 | tf_op jit(solution)/shard_map/ppermute | solution.py:97
  21.6 0.0 copy-done
  21.6 0.6 %multiply_add_fusion = f32[8,1024]{1,0:T(8,128)} fusion(f32[8,1024]{1,0:T(8,128)S(1)} %copy-done, f32[8,1024]{1,0:T(8,128)S(1)} %shard_map.40, f32[8,1024]{1,0:T(8,128)S(1)} %collective-permute-done.4), kind=kLoop, calls=%fused_computation.1 | loop fusion | flops 24576 | bytes 131072 | tf_op jit(solution)/shard_map/add | solution.py:98
  (3 shorter events, 0.0 us)
Async XLA Ops:
  1.5 5.3 %collective-permute-start.3 = (f32[16,1024]{1,0:T(8,128)S(1)}, f32[16,1024]{1,0:T(8,128)S(1)}, u32[]{:S(2)}, u32[]{:S(2)}) collective-permute-start(f32[16,1024]{1,0:T(8,128)S(1)} %pad_maximum_fusion.own_ref), channel_id=1, source_target_pairs={{1,9},{3,11},{5,13},{7,15},{9,1},{11,3},{13,5},{15,7},{17,25},{19,... | collective-permute-start | bytes 196616 | tf_op jit(solution)/shard_map/ppermute | solution.py:92
  2.2 6.9 %collective-permute-start.2 = (f32[16,1024]{1,0:T(8,128)S(1)}, f32[16,1024]{1,0:T(8,128)S(1)}, u32[]{:S(2)}, u32[]{:S(2)}) collective-permute-start(f32[16,1024]{1,0:T(8,128)S(1)} %pad_maximum_fusion.own_ref), channel_id=1, source_target_pairs={{1,11},{3,9},{5,15},{7,13},{9,3},{11,1},{13,7},{15,5},{0,2},{2,0},... | collective-permute-start | bytes 196616 | tf_op jit(solution)/shard_map/ppermute | solution.py:92
  5.2 6.2 %collective-permute-start.1 = (f32[16,1024]{1,0:T(8,128)S(1)}, f32[16,1024]{1,0:T(8,128)S(1)}, u32[]{:S(2)}, u32[]{:S(2)}) collective-permute-start(f32[16,1024]{1,0:T(8,128)S(1)} %pad_maximum_fusion.own_ref), channel_id=1, source_target_pairs={{1,13},{3,15},{5,9},{7,11},{9,5},{11,7},{13,1},{15,3},{0,4},{2,6},... | collective-permute-start | bytes 196616 | tf_op jit(solution)/shard_map/ppermute | solution.py:92
  6.8 6.9 %collective-permute-start = (f32[16,1024]{1,0:T(8,128)S(1)}, f32[16,1024]{1,0:T(8,128)S(1)}, u32[]{:S(2)}, u32[]{:S(2)}) collective-permute-start(f32[16,1024]{1,0:T(8,128)S(1)} %pad_maximum_fusion.own_ref), channel_id=1, source_target_pairs={{1,15},{3,13},{5,11},{7,9},{9,7},{11,5},{13,3},{15,1},{0,6},{2,4},... | collective-permute-start | bytes 196616 | tf_op jit(solution)/shard_map/ppermute | solution.py:92
  13.7 7.8 %copy-start = (f32[8,1024]{1,0:T(8,128)S(1)}, f32[8,1024]{1,0:T(8,128)}, u32[]{:S(2)}) copy-start(f32[8,1024]{1,0:T(8,128)} %param.4) | copy-start | bytes 98308
  16.1 5.5 %collective-permute-start.4 = (f32[8,1024]{1,0:T(8,128)S(1)}, f32[8,1024]{1,0:T(8,128)S(1)}, u32[]{:S(2)}, u32[]{:S(2)}) collective-permute-start(f32[8,1024]{1,0:T(8,128)S(1)} %shard_map.40), channel_id=1, source_target_pairs={{0,1},{1,0},{2,3},{3,2},{4,5},{5,4},{6,7},{7,6},{8,9},{9,8},{10,11... | collective-permute-start | bytes 98312 | tf_op jit(solution)/shard_map/ppermute | solution.py:97

commit v2 on v1

v2 whole, which is shorter than its diff:
```python
import math

import jax
import jax.numpy as jnp
from jax import lax
from jax.experimental import pallas as pl
from jax.experimental.pallas import tpu as pltpu
from jax.sharding import PartitionSpec as P

NOISE = 0.1
LOG2E = math.log2(math.e)
LN2 = math.log(2.0)
POINT_FACTOR = math.sqrt(5.0) * LOG2E
RHS_FACTOR = LN2 * LN2 / 3.0
SHIFT = 1.5 * LOG2E
REST = 0.75 * LOG2E * LOG2E
STEP = 256
DEPTH = 64
VMEM = pl.BlockSpec(memory_space=pltpu.VMEM)


def three_parts(values):
    high = values.astype(jnp.bfloat16).astype(jnp.float32)
    rest = values - high
    middle = rest.astype(jnp.bfloat16).astype(jnp.float32)
    return high, middle, rest - middle


def factors(points, left):
    norms = jnp.sum(points * points, axis=0, keepdims=True)
    high, middle, low = three_parts(-2.0 * points if left else points)
    ones = [jnp.ones_like(norms)] * 3
    rows = [*three_parts(norms), *ones] if left else [*ones, *three_parts(norms)]
    rows.append(jnp.zeros((DEPTH - 54, points.shape[1]), jnp.float32))
    order = [high, high, middle, high, low, middle] if left else [high, middle, high, low, high, middle]
    return jnp.concatenate(order + rows, axis=0)


def multiply(a, b):
    return lax.dot_general(a, b, (((1,), (0,)), ((), ())), preferred_element_type=jnp.float32)


def tile_kernel(count, rows_ref, *refs):
    columns, (before_ref, out_ref, left_ref, total_ref) = refs[:count], refs[count:]
    width = rows_ref.shape[1]
    depth = columns[0].shape[1]
    right = factors(rows_ref[:8] * POINT_FACTOR, False).astype(jnp.bfloat16)
    total_ref[...] = jnp.zeros_like(total_ref)
    for column in columns:
        left_ref[...] = factors(column[:8] * POINT_FACTOR, True).T.astype(jnp.bfloat16)
        values = column[8:] * RHS_FACTOR
        high = values.astype(jnp.bfloat16).astype(jnp.float32)
        both = jnp.concatenate([high, values - high], axis=0).astype(jnp.bfloat16)
        single = jnp.concatenate([high, jnp.zeros_like(high)], axis=0).astype(jnp.bfloat16)
        for j in range(0, depth, STEP):
            for i in range(0, width, STEP):
                squared = jnp.maximum(multiply(left_ref[j : j + STEP], right[:, i : i + STEP]), 1e-30)
                scaled = squared * lax.rsqrt(squared)
                shifted = scaled + SHIFT
                entries = (shifted * shifted + REST) * jnp.exp2(-scaled)
                rounded = entries.astype(jnp.bfloat16)
                remainder = (entries - rounded.astype(jnp.float32)).astype(jnp.bfloat16)
                total_ref[:, i : i + STEP] += multiply(both[:, j : j + STEP], rounded) + multiply(
                    single[:, j : j + STEP], remainder
                )
    out_ref[...] = before_ref[...] + total_ref[:8] + total_ref[8:]


def tiles(rows, columns, before):
    width, depth = rows.shape[1], columns[0].shape[1]
    entries = width * depth * len(columns)
    return pl.pallas_call(
        lambda *refs: tile_kernel(len(columns), *refs),
        out_shape=jax.ShapeDtypeStruct((8, width), jnp.float32),
        in_specs=[VMEM] * (len(columns) + 2),
        out_specs=VMEM,
        scratch_shapes=[pltpu.VMEM((depth, DEPTH), jnp.bfloat16), pltpu.VMEM((16, width), jnp.float32)],
        compiler_params=pltpu.CompilerParams(vmem_limit_bytes=24 * 1024 * 1024),
        cost_estimate=pl.CostEstimate(flops=160 * entries, bytes_accessed=4 * 32 * depth, transcendentals=2 * entries),
    )(rows, *columns, before)


def local(points, rhs, scales):
    block_count = lax.axis_size("blk")
    mine = jnp.concatenate([points / scales[:, None], rhs], axis=0)
    rows = mine[:8]

    def fetch(array, offsets):
        pairs = [(2 * i + s, 2 * (i ^ k) + s) for s, k in enumerate(offsets) if k for i in range(block_count)]
        return lax.ppermute(array, ("blk", "section"), pairs)

    partner_rows = fetch(rows, (1, 1))
    columns = [fetch(mine, (offset, offset + 2)) for offset in range(0, block_count, 4)]
    columns[0] = jnp.where(lax.axis_index("section") == 0, mine, columns[0])
    zeros = jnp.zeros_like(rhs)
    first = tiles(rows, columns[:1], zeros)
    first, again = lax.optimization_barrier((first, zeros))
    for_partner = tiles(partner_rows, columns, again)
    returned = fetch(for_partner, (1, 1))
    total = tiles(rows, columns[1:], first) + returned
    swapped = lax.ppermute(total, "section", [(0, 1), (1, 0)])
    return total + swapped + NOISE * rhs


def solution(mesh):
    in_specs = (P(None, ("parts", "blk")), P(None, ("parts", "blk")), P("parts"))
    out_specs = P(None, ("parts", "blk"))
    return jax.shard_map(local, mesh=mesh, in_specs=in_specs, out_specs=out_specs, check_vma=False)
```

time: 22.4 us -> 20.1 us (0.90)
  starting transfers between devices: 9.92 us -> 8.51 us
  other arithmetic: 2.15 us -> 1.48 us
  Pallas kernels: 9.21 us -> 8.8 us
    ppermute x1, starting transfers between devices: 4.64 us -> 0.69 us  [local(): swapped = lax.ppermute(total, 'section', [(0, 1), (1, 0)])]
    ppermute x4, starting transfers between devices: 5.28 us -> 7.82 us  [fetch(): return lax.ppermute(array, ('blk', 'section'), pairs)]
    mul x1 -> x0, other arithmetic: 0.85 us -> none  [local(): rhs * RHS_FACTOR]
    pallas_call x4 -> x3, Pallas kernels: 9.21 us -> 8.8 us  [tiles(): pl.pallas_call(lambda *refs: tile_kernel(len(columns), *refs), out_shape=...]
  transfers between devices with their start and end apart: 5 -> 5, of which waited for: 1 -> 3; matrix products, arithmetic and copies ran while one was open for 0% -> 0% of each run, Pallas kernels for 31% -> 23%
where the time goes in v2:
time: 20.1 us; the launch traced here: 19.9 us
  Pallas kernels  8.8 us (44%)
  starting transfers between devices  8.51 us (42%)
  other arithmetic  1.48 us (7%)
  waiting for transfers between devices  1.06 us (5%)
    pallas_call x3, Pallas kernels, tiles(): pl.pallas_call(lambda *refs: tile_kernel(len(columns), *refs), out_shape=...  8.8 us
    ppermute x4, starting transfers between devices, fetch(): return lax.ppermute(array, ('blk', 'section'), pairs)  7.82 us
    ppermute x1, waiting for transfers between devices, local(): swapped = lax.ppermute(total, 'section', [(0, 1), (1, 0)])  0.86 us
    div x1, other arithmetic, local(): mine = jnp.concatenate([points / scales[:, None], rhs], axis=0)  0.84 us
    ppermute x1, starting transfers between devices, local(): swapped = lax.ppermute(total, 'section', [(0, 1), (1, 0)])  0.69 us
    add x1, other arithmetic, local(): return total + swapped + NOISE * rhs  0.62 us
  transfers between devices with their start and end apart: 5, of which 3 were waited for; matrix products, arithmetic and copies ran while one was open for 0% of the time, Pallas kernels for 23%

profile of v2, /device:TPU:0, one launch (start us, length us, event | category | flops | bytes accessed | tf_op | source)
XLA Modules:
  0.0 19.9 jit_solution(9497229541063973566)
XLA Ops:
  0.0 0.0 copy-start
  0.0 0.8 %broadcast_divide_fusion.refs_0_ = f32[8,1024]{1,0:T(8,128)S(1)} fusion(f32[8,1024]{1,0:T(8,128)} %param.3, f32[8]{0:T(128)} %param.5), kind=kLoop, calls=%fused_computation.3 | loop fusion | flops 8192 | bytes 65568 | tf_op jit(solution)/shard_map/div | solution.py:85
  0.8 0.0 copy-done
  0.9 0.7 %collective-permute-start.1 = (f32[16,1024]{1,0:T(8,128)S(1)}, f32[16,1024]{1,0:T(8,128)S(1)}, u32[]{:S(2)}, u32[]{:S(2)}) collective-permute-start(f32[16,1024]{1,0:T(8,128)S(1)} %pad_maximum_fusion), channel_id=1, source_target_pairs={{1,5},{3,7},{5,1},{7,3},{9,13},{11,15},{13,9},{15,11},{17,21},{19,... | collective-permute-start | bytes 196616 | tf_op jit(solution)/shard_map/ppermute | solution.py:90
  1.5 4.1 %collective-permute-start = (f32[16,1024]{1,0:T(8,128)S(1)}, f32[16,1024]{1,0:T(8,128)S(1)}, u32[]{:S(2)}, u32[]{:S(2)}) collective-permute-start(f32[16,1024]{1,0:T(8,128)S(1)} %pad_maximum_fusion), channel_id=1, source_target_pairs={{0,8},{2,10},{4,12},{6,14},{8,0},{10,2},{12,4},{14,6},{1,13},{3,15... | collective-permute-start | bytes 196616 | tf_op jit(solution)/shard_map/ppermute | solution.py:90
  5.6 1.5 %collective-permute-start.2 = (f32[8,1024]{1,0:T(8,128)S(1)}, f32[8,1024]{1,0:T(8,128)S(1)}, u32[]{:S(2)}, u32[]{:S(2)}) collective-permute-start(f32[8,1024]{1,0:T(8,128)S(1)} %broadcast_divide_fusion.refs_0_), channel_id=1, source_target_pairs={{0,2},{2,0},{4,6},{6,4},{8,10},{10,8},{12,14},{14,12},{1,3},{3,1},... | collective-permute-start | bytes 98312 | tf_op jit(solution)/shard_map/ppermute | solution.py:90
  7.2 0.0 collective-permute-done.1
  7.2 2.3 %shard_map.37.refs_2_ = f32[8,1024]{1,0:T(8,128)S(1)} custom-call(f32[8,1024]{1,0:T(8,128)S(1)} %broadcast_divide_fusion.refs_0_, f32[16,1024]{1,0:T(8,128)S(1)} %broadcast_select_fusion.refs_1_, f32[8,1024]{1,0:T(8,128)S(1)} %broadcast_in_dim.4.refs_2_.refs_3_), custom_call_target="tpu_custom_call" | custom-call | flops 167772160 | bytes 131072 | tf_op jit(solution)/shard_map/pallas_call | solution.py:72
  9.5 0.1 collective-permute-done.2.refs_0_
  9.5 0.0 collective-permute-done.refs_1_.refs_2_
  9.6 4.2 %shard_map.39 = f32[8,1024]{1,0:T(8,128)S(1)} custom-call(f32[8,1024]{1,0:T(8,128)S(1)} %collective-permute-done.2.refs_0_, f32[16,1024]{1,0:T(8,128)S(1)} %broadcast_select_fusion.refs_1_, f32[16,1024]{1,0:T(8,128)S(1)} %collective-permute-done.refs_1_.refs_2_, f32[8,1024]{1,0:T(8,128)S(1)} %broadcast_in_dim.4.refs_2_.refs_3_), custom_call_target="tpu_custom_call" | custom-call | flops 335544320 | bytes 131072 | tf_op jit(solution)/shard_map/pallas_call | solution.py:72
  13.8 1.5 %collective-permute-start.3 = (f32[8,1024]{1,0:T(8,128)S(1)}, f32[8,1024]{1,0:T(8,128)S(1)}, u32[]{:S(2)}, u32[]{:S(2)}) collective-permute-start(f32[8,1024]{1,0:T(8,128)S(1)} %shard_map.39), channel_id=1, source_target_pairs={{0,2},{2,0},{4,6},{6,4},{8,10},{10,8},{12,14},{14,12},{1,3},{3,1},... | collective-permute-start | bytes 98312 | tf_op jit(solution)/shard_map/ppermute | solution.py:90
  15.3 2.3 %shard_map.38 = f32[8,1024]{1,0:T(8,128)S(1)} custom-call(f32[8,1024]{1,0:T(8,128)S(1)} %broadcast_divide_fusion.refs_0_, f32[16,1024]{1,0:T(8,128)S(1)} %collective-permute-done.refs_1_.refs_2_, f32[8,1024]{1,0:T(8,128)S(1)} %shard_map.37.refs_2_), custom_call_target="tpu_custom_call" | custom-call | flops 167772160 | bytes 131072 | tf_op jit(solution)/shard_map/pallas_call | solution.py:72
  17.6 0.1 collective-permute-done.3
  17.7 0.7 %collective-permute-start.4 = (f32[8,1024]{1,0:T(8,128)S(1)}, f32[8,1024]{1,0:T(8,128)S(1)}, u32[]{:S(2)}, u32[]{:S(2)}) collective-permute-start(f32[8,1024]{1,0:T(8,128)S(1)} %add.9), channel_id=1, source_target_pairs={{0,1},{1,0},{2,3},{3,2},{4,5},{5,4},{6,7},{7,6},{8,9},{9,8},{10,11... | collective-permute-start | bytes 98312 | tf_op jit(solution)/shard_map/ppermute | solution.py:101
  18.4 0.9 %collective-permute-done.4 = f32[8,1024]{1,0:T(8,128)S(1)} collective-permute-done((f32[8,1024]{1,0:T(8,128)S(1)}, f32[8,1024]{1,0:T(8,128)S(1)}, u32[]{:S(2)}, u32[]{:S(2)}) %collective-permute-start.4) | collective-permute-done | bytes 32800 | tf_op jit(solution)/shard_map/ppermute | solution.py:101
  19.3 0.6 %multiply_add_fusion = f32[8,1024]{1,0:T(8,128)} fusion(f32[8,1024]{1,0:T(8,128)S(1)} %copy-done, f32[8,1024]{1,0:T(8,128)S(1)} %add.9, f32[8,1024]{1,0:T(8,128)S(1)} %collective-permute-done.4), kind=kLoop, calls=%fused_computation.1 | loop fusion | flops 24576 | bytes 131072 | tf_op jit(solution)/shard_map/add | solution.py:102
  (4 shorter events, 0.0 us)
Async XLA Ops:
  0.0 0.8 %copy-start = (f32[8,1024]{1,0:T(8,128)S(1)}, f32[8,1024]{1,0:T(8,128)}, u32[]{:S(2)}) copy-start(f32[8,1024]{1,0:T(8,128)} %param.4) | copy-start | bytes 98308
  0.9 6.3 %collective-permute-start.1 = (f32[16,1024]{1,0:T(8,128)S(1)}, f32[16,1024]{1,0:T(8,128)S(1)}, u32[]{:S(2)}, u32[]{:S(2)}) collective-permute-start(f32[16,1024]{1,0:T(8,128)S(1)} %pad_maximum_fusion), channel_id=1, source_target_pairs={{1,5},{3,7},{5,1},{7,3},{9,13},{11,15},{13,9},{15,11},{17,21},{19,... | collective-permute-start | bytes 196616 | tf_op jit(solution)/shard_map/ppermute | solution.py:90
  1.5 8.0 %collective-permute-start = (f32[16,1024]{1,0:T(8,128)S(1)}, f32[16,1024]{1,0:T(8,128)S(1)}, u32[]{:S(2)}, u32[]{:S(2)}) collective-permute-start(f32[16,1024]{1,0:T(8,128)S(1)} %pad_maximum_fusion), channel_id=1, source_target_pairs={{0,8},{2,10},{4,12},{6,14},{8,0},{10,2},{12,4},{14,6},{1,13},{3,15... | collective-permute-start | bytes 196616 | tf_op jit(solution)/shard_map/ppermute | solution.py:90
  5.6 3.9 %collective-permute-start.2 = (f32[8,1024]{1,0:T(8,128)S(1)}, f32[8,1024]{1,0:T(8,128)S(1)}, u32[]{:S(2)}, u32[]{:S(2)}) collective-permute-start(f32[8,1024]{1,0:T(8,128)S(1)} %broadcast_divide_fusion.refs_0_), channel_id=1, source_target_pairs={{0,2},{2,0},{4,6},{6,4},{8,10},{10,8},{12,14},{14,12},{1,3},{3,1},... | collective-permute-start | bytes 98312 | tf_op jit(solution)/shard_map/ppermute | solution.py:90
  13.8 3.9 %collective-permute-start.3 = (f32[8,1024]{1,0:T(8,128)S(1)}, f32[8,1024]{1,0:T(8,128)S(1)}, u32[]{:S(2)}, u32[]{:S(2)}) collective-permute-start(f32[8,1024]{1,0:T(8,128)S(1)} %shard_map.39), channel_id=1, source_target_pairs={{0,2},{2,0},{4,6},{6,4},{8,10},{10,8},{12,14},{14,12},{1,3},{3,1},... | collective-permute-start | bytes 98312 | tf_op jit(solution)/shard_map/ppermute | solution.py:90
  17.7 1.6 %collective-permute-start.4 = (f32[8,1024]{1,0:T(8,128)S(1)}, f32[8,1024]{1,0:T(8,128)S(1)}, u32[]{:S(2)}, u32[]{:S(2)}) collective-permute-start(f32[8,1024]{1,0:T(8,128)S(1)} %add.9), channel_id=1, source_target_pairs={{0,1},{1,0},{2,3},{3,2},{4,5},{5,4},{6,7},{7,6},{8,9},{9,8},{10,11... | collective-permute-start | bytes 98312 | tf_op jit(solution)/shard_map/ppermute | solution.py:101

commit v3 on v2

v3 whole, which is shorter than its diff:
```python
import math

import jax
import jax.numpy as jnp
from jax import lax
from jax.experimental import pallas as pl
from jax.experimental.pallas import tpu as pltpu
from jax.sharding import PartitionSpec as P

NOISE = 0.1
POINT_FACTOR = math.sqrt(5.0) / 3.0
RHS_FACTOR = 3.0
DECAY = -3.0 * math.log2(math.e)
STEP = 256
DEPTH = 64
VMEM = pl.BlockSpec(memory_space=pltpu.VMEM)


def three_parts(values):
    high = values.astype(jnp.bfloat16).astype(jnp.float32)
    rest = values - high
    middle = rest.astype(jnp.bfloat16).astype(jnp.float32)
    return high, middle, rest - middle


def factors(points, left):
    norms = jnp.sum(points * points, axis=0, keepdims=True)
    high, middle, low = three_parts(-2.0 * points if left else points)
    ones = [jnp.ones_like(norms)] * 3
    rows = [*three_parts(norms), *ones] if left else [*ones, *three_parts(norms)]
    rows.append(jnp.zeros((DEPTH - 54, points.shape[1]), jnp.float32))
    order = [high, high, middle, high, low, middle] if left else [high, middle, high, low, high, middle]
    return jnp.concatenate(order + rows, axis=0)


def multiply(a, b):
    return lax.dot_general(a, b, (((1,), (0,)), ((), ())), preferred_element_type=jnp.float32)


def tile_kernel(known, made, *refs):
    rows_ref, refs = refs[0], refs[1:]
    columns, refs = refs[: known + made], refs[known + made :]
    lefts, refs = refs[:known], refs[known:]
    before_ref, out_ref, refs = refs[0], refs[1], refs[2:]
    lefts, refs = [*lefts, *refs[:made]], refs[made:]
    total_ref = refs[-1]
    right_ref = rows_ref
    if rows_ref.dtype == jnp.float32:
        right_ref = refs[0]
        right_ref[...] = factors(rows_ref[:8] * POINT_FACTOR, False).astype(jnp.bfloat16)
    total_ref[...] = jnp.zeros_like(total_ref)
    for n, (column, left_ref) in enumerate(zip(columns, lefts)):
        if n >= known:
            left_ref[...] = factors(column[:8] * POINT_FACTOR, True).T.astype(jnp.bfloat16)
        values = column[8:] * RHS_FACTOR
        high = values.astype(jnp.bfloat16).astype(jnp.float32)
        both = jnp.concatenate([high, values - high], axis=0).astype(jnp.bfloat16)
        single = jnp.concatenate([high, jnp.zeros_like(high)], axis=0).astype(jnp.bfloat16)
        for j in range(0, column.shape[1], STEP):
            for i in range(0, right_ref.shape[1], STEP):
                product = multiply(left_ref[j : j + STEP], right_ref[:, i : i + STEP])
                squared = jnp.maximum(product, 1e-30)
                scaled = squared * lax.rsqrt(squared)
                entries = (squared + (scaled + 1.0 / 3.0)) * jnp.exp2(scaled * DECAY)
                rounded = entries.astype(jnp.bfloat16)
                remainder = (entries - rounded.astype(jnp.float32)).astype(jnp.bfloat16)
                total_ref[:, i : i + STEP] += multiply(both[:, j : j + STEP], rounded) + multiply(
                    single[:, j : j + STEP], remainder
                )
    out_ref[...] = before_ref[...] + total_ref[:8] + total_ref[8:]


def tiles(rows, columns, lefts, before):
    width, depth = rows.shape[1], columns[0].shape[1]
    known, made = len(lefts), len(columns) - len(lefts)
    fresh = rows.dtype == jnp.float32
    entries = width * depth * len(columns)
    out, *new = pl.pallas_call(
        lambda *refs: tile_kernel(known, made, *refs),
        out_shape=[jax.ShapeDtypeStruct((8, width), jnp.float32)]
        + [jax.ShapeDtypeStruct((depth, DEPTH), jnp.bfloat16)] * made
        + [jax.ShapeDtypeStruct((DEPTH, width), jnp.bfloat16)] * fresh,
        in_specs=[VMEM] * (2 + known + len(columns)),
        out_specs=[VMEM] * (1 + made + fresh),
        scratch_shapes=[pltpu.VMEM((16, width), jnp.float32)],
        compiler_params=pltpu.CompilerParams(vmem_limit_bytes=24 * 1024 * 1024),
        cost_estimate=pl.CostEstimate(flops=160 * entries, bytes_accessed=4 * 32 * depth, transcendentals=2 * entries),
    )(rows, *columns, *lefts, before)
    return out, new.pop() if fresh else rows, [*lefts, *new]


def local(points, rhs, scales):
    block_count = lax.axis_size("blk")
    mine = jnp.concatenate([points / scales[:, None], rhs], axis=0)

    def fetch(array, offsets):
        pairs = [(2 * i + s, 2 * (i ^ k) + s) for s, k in enumerate(offsets) if k for i in range(block_count)]
        return lax.ppermute(array, ("blk", "section"), pairs)

    partner_rows = fetch(mine, (1, 1))
    columns = [fetch(mine, (offset, offset + 2)) for offset in range(0, block_count, 4)]
    columns[0] = jnp.where(lax.axis_index("section") == 0, mine, columns[0])
    zeros = jnp.zeros_like(rhs)
    first, right, lefts = tiles(mine[:8], columns[:1], [], zeros)
    first, again = lax.optimization_barrier((first, zeros))
    for_partner, _, lefts = tiles(partner_rows[:8], columns, lefts, again)
    returned = fetch(for_partner, (1, 1))
    total, _, _ = tiles(right, columns[1:], lefts[1:], first)
    total = total + returned
    swapped = lax.ppermute(total, "section", [(0, 1), (1, 0)])
    return total + swapped + NOISE * rhs


def solution(mesh):
    in_specs = (P(None, ("parts", "blk")), P(None, ("parts", "blk")), P("parts"))
    out_specs = P(None, ("parts", "blk"))
    return jax.shard_map(local, mesh=mesh, in_specs=in_specs, out_specs=out_specs, check_vma=False)
```

time: 20.1 us -> 19.7 us (0.980)
  waiting for transfers between devices: 1.06 us -> 2.63 us
  Pallas kernels: 8.8 us -> 7.43 us
  starting transfers between devices: 8.51 us -> 7.93 us
    pallas_call x3, Pallas kernels: 8.8 us -> 7.43 us  [tiles(): pl.pallas_call(lambda *refs: tile_kernel(known, made, *refs), out_shape=[...]
    ppermute x4, waiting for transfers between devices: 0.2 us -> 1.54 us  [fetch(): return lax.ppermute(array, ('blk', 'section'), pairs)]
    ppermute x1, starting transfers between devices: 0.69 us -> 0.12 us  [local(): swapped = lax.ppermute(total, 'section', [(0, 1), (1, 0)])]
    ppermute x1, waiting for transfers between devices: 0.86 us -> 1.09 us  [local(): swapped = lax.ppermute(total, 'section', [(0, 1), (1, 0)])]
  transfers between devices with their start and end apart: 5 -> 5, of which waited for: 3 -> 3; matrix products, arithmetic and copies ran while one was open for 0% -> 0% of each run, Pallas kernels for 23% -> 20%
where the time goes in v3:
time: 19.7 us; the launch traced here: 19.5 us
  starting transfers between devices  7.93 us (40%)
  Pallas kernels  7.43 us (38%)
  waiting for transfers between devices  2.63 us (13%)
  other arithmetic  1.48 us (8%)
    ppermute x4, starting transfers between devices, fetch(): return lax.ppermute(array, ('blk', 'section'), pairs)  7.82 us
    pallas_call x3, Pallas kernels, tiles(): pl.pallas_call(lambda *refs: tile_kernel(known, made, *refs), out_shape=[...  7.43 us
    ppermute x4, waiting for transfers between devices, fetch(): return lax.ppermute(array, ('blk', 'section'), pairs)  1.54 us
    ppermute x1, waiting for transfers between devices, local(): swapped = lax.ppermute(total, 'section', [(0, 1), (1, 0)])  1.09 us
    div x1, other arithmetic, local(): mine = jnp.concatenate([points / scales[:, None], rhs], axis=0)  0.84 us
    add x1, other arithmetic, local(): return total + swapped + NOISE * rhs  0.62 us
  transfers between devices with their start and end apart: 5, of which 3 were waited for; matrix products, arithmetic and copies ran while one was open for 0% of the time, Pallas kernels for 20%

profile of v3, /device:TPU:0, one launch (start us, length us, event | category | flops | bytes accessed | tf_op | source)
XLA Modules:
  0.0 19.5 jit_solution(1882300647632822172)
XLA Ops:
  0.0 0.0 copy-start
  0.0 0.8 %broadcast_divide_fusion.refs_0_ = f32[8,1024]{1,0:T(8,128)S(1)} fusion(f32[8,1024]{1,0:T(8,128)} %param.3, f32[8]{0:T(128)} %param.5), kind=kLoop, calls=%fused_computation.3 | loop fusion | flops 8192 | bytes 65568 | tf_op jit(solution)/shard_map/div | solution.py:94
  0.8 0.0 copy-done
  0.9 0.7 %collective-permute-start = (f32[16,1024]{1,0:T(8,128)S(1)}, f32[16,1024]{1,0:T(8,128)S(1)}, u32[]{:S(2)}, u32[]{:S(2)}) collective-permute-start(f32[16,1024]{1,0:T(8,128)S(1)} %pad_maximum_fusion), channel_id=1, source_target_pairs={{1,5},{3,7},{5,1},{7,3},{9,13},{11,15},{13,9},{15,11},{17,21},{19,... | collective-permute-start | bytes 196616 | tf_op jit(solution)/shard_map/ppermute | solution.py:98
  1.5 4.1 %collective-permute-start.1 = (f32[16,1024]{1,0:T(8,128)S(1)}, f32[16,1024]{1,0:T(8,128)S(1)}, u32[]{:S(2)}, u32[]{:S(2)}) collective-permute-start(f32[16,1024]{1,0:T(8,128)S(1)} %pad_maximum_fusion), channel_id=1, source_target_pairs={{0,8},{2,10},{4,12},{6,14},{8,0},{10,2},{12,4},{14,6},{1,13},{3,15... | collective-permute-start | bytes 196616 | tf_op jit(solution)/shard_map/ppermute | solution.py:98
  5.6 1.5 %collective-permute-start.2 = (f32[16,1024]{1,0:T(8,128)S(1)}, f32[16,1024]{1,0:T(8,128)S(1)}, u32[]{:S(2)}, u32[]{:S(2)}) collective-permute-start(f32[16,1024]{1,0:T(8,128)S(1)} %pad_maximum_fusion), channel_id=1, source_target_pairs={{0,2},{2,0},{4,6},{6,4},{8,10},{10,8},{12,14},{14,12},{1,3},{3,1},... | collective-permute-start | bytes 196616 | tf_op jit(solution)/shard_map/ppermute | solution.py:98
  7.2 0.0 collective-permute-done
  7.2 2.0 %shard_map.37 = (f32[8,1024]{1,0:T(8,128)S(1)}, bf16[1024,64]{1,0:T(8,128)(2,1)S(1)}, bf16[64,1024]{1,0:T(8,128)(2,1)S(1)}) custom-call(f32[8,1024]{1,0:T(8,128)S(1)} %broadcast_divide_fusion.refs_0_, f32[16,1024]{1,0:T(8,128)S(1)} %broadcast_select_fusion.refs_1_, f32[8,1024]{1,0:T(8,128)S(1)} %broadcast_in_dim.4.refs_2_.refs_4_), custom_call_target="tpu_custom_call" | custom-call | flops 167772160 | bytes 131072 | tf_op jit(solution)/shard_map/pallas_call | solution.py:78
  9.2 0.7 %collective-permute-done.2 = f32[16,1024]{1,0:T(8,128)S(1)} collective-permute-done((f32[16,1024]{1,0:T(8,128)S(1)}, f32[16,1024]{1,0:T(8,128)S(1)}, u32[]{:S(2)}, u32[]{:S(2)}) %collective-permute-start.2) | collective-permute-done | bytes 65568 | tf_op jit(solution)/shard_map/ppermute | solution.py:98
  9.9 0.0 collective-permute-done.1.refs_2_.refs_1_
  9.9 3.6 %shard_map.38 = (f32[8,1024]{1,0:T(8,128)S(1)}, bf16[1024,64]{1,0:T(8,128)(2,1)S(1)}, bf16[64,1024]{1,0:T(8,128)(2,1)}) custom-call(f32[8,1024]{1,0:T(8,128)S(1)} %slice.4.refs_0_, f32[16,1024]{1,0:T(8,128)S(1)} %broadcast_select_fusion.refs_1_, f32[16,1024]{1,0:T(8,128)S(1)} %collective-permute-done.1.refs_2_.refs_1_, ...), custom_call_target="tpu_custom_call" | custom-call | flops 335544320 | bytes 131072 | tf_op jit(solution)/shard_map/pallas_call | solution.py:78
  13.5 1.5 %collective-permute-start.3 = (f32[8,1024]{1,0:T(8,128)S(1)}, f32[8,1024]{1,0:T(8,128)S(1)}, u32[]{:S(2)}, u32[]{:S(2)}) collective-permute-start(f32[8,1024]{1,0:T(8,128)S(1)} %get-tuple-element.18), channel_id=1, source_target_pairs={{0,2},{2,0},{4,6},{6,4},{8,10},{10,8},{12,14},{14,12},{1,3},{3,1},... | collective-permute-start | bytes 98312 | tf_op jit(solution)/shard_map/ppermute | solution.py:98
  15.0 1.9 %shard_map.39 = f32[8,1024]{1,0:T(8,128)S(1)} custom-call(bf16[64,1024]{1,0:T(8,128)(2,1)S(1)} %get-tuple-element.12.refs_0_, f32[16,1024]{1,0:T(8,128)S(1)} %collective-permute-done.1.refs_2_.refs_1_, bf16[1024,64]{1,0:T(8,128)(2,1)S(1)} %get-tuple-element.16.refs_2_, f32[8,1024]{1,0:T(8,128)S(1)} %get-tuple-element.17.refs_3_), custom_call_target="tpu_custom_call" | custom-call | flops 167772160 | bytes 131072 | tf_op jit(solution)/shard_map/pallas_call | solution.py:78
  16.9 0.8 %collective-permute-done.3 = f32[8,1024]{1,0:T(8,128)S(1)} collective-permute-done((f32[8,1024]{1,0:T(8,128)S(1)}, f32[8,1024]{1,0:T(8,128)S(1)}, u32[]{:S(2)}, u32[]{:S(2)}) %collective-permute-start.3) | collective-permute-done | bytes 32800 | tf_op jit(solution)/shard_map/ppermute | solution.py:98
  17.7 0.1 collective-permute-start.4
  17.8 1.1 %collective-permute-done.4 = f32[8,1024]{1,0:T(8,128)S(1)} collective-permute-done((f32[8,1024]{1,0:T(8,128)S(1)}, f32[8,1024]{1,0:T(8,128)S(1)}, u32[]{:S(2)}, u32[]{:S(2)}) %collective-permute-start.4) | collective-permute-done | bytes 32800 | tf_op jit(solution)/shard_map/ppermute | solution.py:110
  18.9 0.6 %multiply_add_fusion = f32[8,1024]{1,0:T(8,128)} fusion(f32[8,1024]{1,0:T(8,128)S(1)} %copy-done, f32[8,1024]{1,0:T(8,128)S(1)} %add.9, f32[8,1024]{1,0:T(8,128)S(1)} %collective-permute-done.4), kind=kLoop, calls=%fused_computation.1 | loop fusion | flops 24576 | bytes 131072 | tf_op jit(solution)/shard_map/add | solution.py:111
  (5 shorter events, 0.0 us)
Async XLA Ops:
  0.0 0.8 %copy-start = (f32[8,1024]{1,0:T(8,128)S(1)}, f32[8,1024]{1,0:T(8,128)}, u32[]{:S(2)}) copy-start(f32[8,1024]{1,0:T(8,128)} %param.4) | copy-start | bytes 98308
  0.9 6.3 %collective-permute-start = (f32[16,1024]{1,0:T(8,128)S(1)}, f32[16,1024]{1,0:T(8,128)S(1)}, u32[]{:S(2)}, u32[]{:S(2)}) collective-permute-start(f32[16,1024]{1,0:T(8,128)S(1)} %pad_maximum_fusion), channel_id=1, source_target_pairs={{1,5},{3,7},{5,1},{7,3},{9,13},{11,15},{13,9},{15,11},{17,21},{19,... | collective-permute-start | bytes 196616 | tf_op jit(solution)/shard_map/ppermute | solution.py:98
  1.5 8.4 %collective-permute-start.1 = (f32[16,1024]{1,0:T(8,128)S(1)}, f32[16,1024]{1,0:T(8,128)S(1)}, u32[]{:S(2)}, u32[]{:S(2)}) collective-permute-start(f32[16,1024]{1,0:T(8,128)S(1)} %pad_maximum_fusion), channel_id=1, source_target_pairs={{0,8},{2,10},{4,12},{6,14},{8,0},{10,2},{12,4},{14,6},{1,13},{3,15... | collective-permute-start | bytes 196616 | tf_op jit(solution)/shard_map/ppermute | solution.py:98
  5.6 4.3 %collective-permute-start.2 = (f32[16,1024]{1,0:T(8,128)S(1)}, f32[16,1024]{1,0:T(8,128)S(1)}, u32[]{:S(2)}, u32[]{:S(2)}) collective-permute-start(f32[16,1024]{1,0:T(8,128)S(1)} %pad_maximum_fusion), channel_id=1, source_target_pairs={{0,2},{2,0},{4,6},{6,4},{8,10},{10,8},{12,14},{14,12},{1,3},{3,1},... | collective-permute-start | bytes 196616 | tf_op jit(solution)/shard_map/ppermute | solution.py:98
  13.5 4.2 %collective-permute-start.3 = (f32[8,1024]{1,0:T(8,128)S(1)}, f32[8,1024]{1,0:T(8,128)S(1)}, u32[]{:S(2)}, u32[]{:S(2)}) collective-permute-start(f32[8,1024]{1,0:T(8,128)S(1)} %get-tuple-element.18), channel_id=1, source_target_pairs={{0,2},{2,0},{4,6},{6,4},{8,10},{10,8},{12,14},{14,12},{1,3},{3,1},... | collective-permute-start | bytes 98312 | tf_op jit(solution)/shard_map/ppermute | solution.py:98
  17.7 1.2 %collective-permute-start.4 = (f32[8,1024]{1,0:T(8,128)S(1)}, f32[8,1024]{1,0:T(8,128)S(1)}, u32[]{:S(2)}, u32[]{:S(2)}) collective-permute-start(f32[8,1024]{1,0:T(8,128)S(1)} %add.9), channel_id=1, source_target_pairs={{0,1},{1,0},{2,3},{3,2},{4,5},{5,4},{6,7},{7,6},{8,9},{9,8},{10,11... | collective-permute-start | bytes 98312 | tf_op jit(solution)/shard_map/ppermute | solution.py:110

commit v4 on v3

--- a/solution.py
+++ b/solution.py
@@ -94,21 +94,26 @@
     mine = jnp.concatenate([points / scales[:, None], rhs], axis=0)
 
     def fetch(array, offsets):
-        pairs = [(2 * i + s, 2 * (i ^ k) + s) for s, k in enumerate(offsets) if k for i in range(block_count)]
+        pairs = [(2 * i + s, 2 * (i ^ k) + s) for s, k in enumerate(offsets) for i in range(block_count)]
         return lax.ppermute(array, ("blk", "section"), pairs)
 
-    partner_rows = fetch(mine, (1, 1))
-    columns = [fetch(mine, (offset, offset + 2)) for offset in range(0, block_count, 4)]
-    columns[0] = jnp.where(lax.axis_index("section") == 0, mine, columns[0])
+    def swap(array):
+        return lax.ppermute(array, "section", [(0, 1), (1, 0)])
+
+    first_section = lax.axis_index("section") == 0
+    offsets = [1, *range(2, block_count, 2)]
+    half = block_count // 4
+    columns = [fetch(mine, pair) for pair in zip(offsets[:half], offsets[half:])]
+    given_rows = swap(columns[0][:8])
     zeros = jnp.zeros_like(rhs)
     first, right, lefts = tiles(mine[:8], columns[:1], [], zeros)
-    first, again = lax.optimization_barrier((first, zeros))
-    for_partner, _, lefts = tiles(partner_rows[:8], columns, lefts, again)
+    first, again, *columns[1:] = lax.optimization_barrier((first, zeros, *columns[1:]))
+    partner_rows = jnp.where(first_section, columns[0][:8], given_rows)
+    for_partner, _, lefts = tiles(partner_rows, columns, lefts, again)
     returned = fetch(for_partner, (1, 1))
     total, _, _ = tiles(right, columns[1:], lefts[1:], first)
     total = total + returned
-    swapped = lax.ppermute(total, "section", [(0, 1), (1, 0)])
-    return total + swapped + NOISE * rhs
+    return total + swap(total) + NOISE * rhs
 
 
 def solution(mesh):

time: 19.7 us -> 18.1 us (0.919)
  waiting for transfers between devices: 2.63 us -> 1.59 us
  starting transfers between devices: 7.93 us -> 7.41 us
    ppermute x4 -> x3, starting transfers between devices: 7.82 us -> 6.62 us  [fetch(): return lax.ppermute(array, ('blk', 'section'), pairs)]
    ppermute x4 -> x3, waiting for transfers between devices: 1.54 us -> 0.72 us  [fetch(): return lax.ppermute(array, ('blk', 'section'), pairs)]
    ppermute x1 -> x2, starting transfers between devices: 0.12 us -> 0.8 us  [swap(): return lax.ppermute(array, 'section', [(0, 1), (1, 0)])]
    ppermute x1 -> x2, waiting for transfers between devices: 1.09 us -> 0.87 us  [swap(): return lax.ppermute(array, 'section', [(0, 1), (1, 0)])]
  transfers between devices with their start and end apart: 5 -> 5, of which waited for: 3 -> 3; matrix products, arithmetic and copies ran while one was open for 0% -> 0% of each run, Pallas kernels for 20% -> 22%
where the time goes in v4:
time: 18.1 us; the launch traced here: 18 us
  Pallas kernels  7.44 us (41%)
  starting transfers between devices  7.41 us (41%)
  waiting for transfers between devices  1.59 us (9%)
  other arithmetic  1.48 us (8%)
    pallas_call x3, Pallas kernels, tiles(): pl.pallas_call(lambda *refs: tile_kernel(known, made, *refs), out_shape=[...  7.44 us
    ppermute x3, starting transfers between devices, fetch(): return lax.ppermute(array, ('blk', 'section'), pairs)  6.62 us
    ppermute x2, waiting for transfers between devices, swap(): return lax.ppermute(array, 'section', [(0, 1), (1, 0)])  0.87 us
    div x1, other arithmetic, local(): mine = jnp.concatenate([points / scales[:, None], rhs], axis=0)  0.84 us
    ppermute x2, starting transfers between devices, swap(): return lax.ppermute(array, 'section', [(0, 1), (1, 0)])  0.8 us
    ppermute x3, waiting for transfers between devices, fetch(): return lax.ppermute(array, ('blk', 'section'), pairs)  0.72 us
    add x1, other arithmetic, local(): return total + swap(total) + NOISE * rhs  0.62 us
  transfers between devices with their start and end apart: 5, of which 3 were waited for; matrix products, arithmetic and copies ran while one was open for 0% of the time, Pallas kernels for 22%

profile of v4, /device:TPU:0, one launch (start us, length us, event | category | flops | bytes accessed | tf_op | source)
XLA Modules:
  0.0 18.0 jit_solution(17641926491803616335)
XLA Ops:
  0.0 0.0 copy-start
  0.0 0.8 %broadcast_divide_fusion.refs_0_ = f32[8,1024]{1,0:T(8,128)S(1)} fusion(f32[8,1024]{1,0:T(8,128)} %param.3, f32[8]{0:T(128)} %param.5), kind=kLoop, calls=%fused_computation.2 | loop fusion | flops 8192 | bytes 65568 | tf_op jit(solution)/shard_map/div | solution.py:94
  0.8 0.0 copy-done
  0.9 3.0 %collective-permute-start = (f32[16,1024]{1,0:T(8,128)S(1)}, f32[16,1024]{1,0:T(8,128)S(1)}, u32[]{:S(2)}, u32[]{:S(2)}) collective-permute-start(f32[16,1024]{1,0:T(8,128)S(1)} %pad_maximum_fusion), channel_id=1, source_target_pairs={{0,2},{2,0},{4,6},{6,4},{8,10},{10,8},{12,14},{14,12},{1,9},{3,11}... | collective-permute-start | bytes 196616 | tf_op jit(solution)/shard_map/ppermute | solution.py:98
  3.9 1.6 %collective-permute-start.1 = (f32[16,1024]{1,0:T(8,128)S(1)}, f32[16,1024]{1,0:T(8,128)S(1)}, u32[]{:S(2)}, u32[]{:S(2)}) collective-permute-start(f32[16,1024]{1,0:T(8,128)S(1)} %pad_maximum_fusion), channel_id=1, source_target_pairs={{0,4},{2,6},{4,0},{6,2},{8,12},{10,14},{12,8},{14,10},{1,13},{3,15... | collective-permute-start | bytes 196616 | tf_op jit(solution)/shard_map/ppermute | solution.py:98
  5.5 0.7 %collective-permute-done.refs_1_ = f32[16,1024]{1,0:T(8,128)S(1)} collective-permute-done((f32[16,1024]{1,0:T(8,128)S(1)}, f32[16,1024]{1,0:T(8,128)S(1)}, u32[]{:S(2)}, u32[]{:S(2)}) %collective-permute-start) | collective-permute-done | bytes 65568 | tf_op jit(solution)/shard_map/ppermute | solution.py:98
  6.1 0.0 collective-permute-start.2
  6.2 2.0 %shard_map.37 = (f32[8,1024]{1,0:T(8,128)S(1)}, bf16[1024,64]{1,0:T(8,128)(2,1)S(1)}, bf16[64,1024]{1,0:T(8,128)(2,1)S(1)}) custom-call(f32[8,1024]{1,0:T(8,128)S(1)} %broadcast_divide_fusion.refs_0_, f32[16,1024]{1,0:T(8,128)S(1)} %collective-permute-done.refs_1_, f32[8,1024]{1,0:T(8,128)S(1)} %broadcast_in_dim.4.refs_2_.refs_4_), custom_call_target="tpu_custom_call" | custom-call | flops 167772160 | bytes 131072 | tf_op jit(solution)/shard_map/pallas_call | solution.py:78
  8.2 0.0 collective-permute-done.1.refs_2_.refs_1_
  8.2 0.0 collective-permute-done.2
  8.2 3.6 %shard_map.38 = (f32[8,1024]{1,0:T(8,128)S(1)}, bf16[1024,64]{1,0:T(8,128)(2,1)S(1)}, bf16[64,1024]{1,0:T(8,128)(2,1)}) custom-call(f32[8,1024]{1,0:T(8,128)S(1)} %broadcast_select_fusion.refs_0_, f32[16,1024]{1,0:T(8,128)S(1)} %collective-permute-done.refs_1_, f32[16,1024]{1,0:T(8,128)S(1)} %collective-permute-done.1.refs_2_.refs_1_, ...), custom_call_target="tpu_custom_call" | custom-call | flops 335544320 | bytes 131072 | tf_op jit(solution)/shard_map/pallas_call | solution.py:78
  11.8 2.0 %collective-permute-start.3 = (f32[8,1024]{1,0:T(8,128)S(1)}, f32[8,1024]{1,0:T(8,128)S(1)}, u32[]{:S(2)}, u32[]{:S(2)}) collective-permute-start(f32[8,1024]{1,0:T(8,128)S(1)} %get-tuple-element.20), channel_id=1, source_target_pairs={{0,2},{2,0},{4,6},{6,4},{8,10},{10,8},{12,14},{14,12},{1,3},{3,1},... | collective-permute-start | bytes 98312 | tf_op jit(solution)/shard_map/ppermute | solution.py:98
  13.8 1.9 %shard_map.39 = f32[8,1024]{1,0:T(8,128)S(1)} custom-call(bf16[64,1024]{1,0:T(8,128)(2,1)S(1)} %get-tuple-element.13.refs_0_, f32[16,1024]{1,0:T(8,128)S(1)} %collective-permute-done.1.refs_2_.refs_1_, bf16[1024,64]{1,0:T(8,128)(2,1)S(1)} %get-tuple-element.18.refs_2_, f32[8,1024]{1,0:T(8,128)S(1)} %get-tuple-element.19.refs_3_), custom_call_target="tpu_custom_call" | custom-call | flops 167772160 | bytes 131072 | tf_op jit(solution)/shard_map/pallas_call | solution.py:78
  15.7 0.1 collective-permute-done.3
  15.7 0.8 %collective-permute-start.4 = (f32[8,1024]{1,0:T(8,128)S(1)}, f32[8,1024]{1,0:T(8,128)S(1)}, u32[]{:S(2)}, u32[]{:S(2)}) collective-permute-start(f32[8,1024]{1,0:T(8,128)S(1)} %add.9), channel_id=1, source_target_pairs={{0,1},{1,0},{2,3},{3,2},{4,5},{5,4},{6,7},{7,6},{8,9},{9,8},{10,11... | collective-permute-start | bytes 98312 | tf_op jit(solution)/shard_map/ppermute | solution.py:101
  16.5 0.9 %collective-permute-done.4 = f32[8,1024]{1,0:T(8,128)S(1)} collective-permute-done((f32[8,1024]{1,0:T(8,128)S(1)}, f32[8,1024]{1,0:T(8,128)S(1)}, u32[]{:S(2)}, u32[]{:S(2)}) %collective-permute-start.4) | collective-permute-done | bytes 32800 | tf_op jit(solution)/shard_map/ppermute | solution.py:101
  17.3 0.6 %multiply_add_fusion = f32[8,1024]{1,0:T(8,128)} fusion(f32[8,1024]{1,0:T(8,128)S(1)} %copy-done, f32[8,1024]{1,0:T(8,128)S(1)} %add.9, f32[8,1024]{1,0:T(8,128)S(1)} %collective-permute-done.4), kind=kLoop, calls=%fused_computation.1 | loop fusion | flops 24576 | bytes 131072 | tf_op jit(solution)/shard_map/add | solution.py:116
  (5 shorter events, 0.0 us)
Async XLA Ops:
  0.0 0.8 %copy-start = (f32[8,1024]{1,0:T(8,128)S(1)}, f32[8,1024]{1,0:T(8,128)}, u32[]{:S(2)}) copy-start(f32[8,1024]{1,0:T(8,128)} %param.4) | copy-start | bytes 98308
  0.9 5.3 %collective-permute-start = (f32[16,1024]{1,0:T(8,128)S(1)}, f32[16,1024]{1,0:T(8,128)S(1)}, u32[]{:S(2)}, u32[]{:S(2)}) collective-permute-start(f32[16,1024]{1,0:T(8,128)S(1)} %pad_maximum_fusion), channel_id=1, source_target_pairs={{0,2},{2,0},{4,6},{6,4},{8,10},{10,8},{12,14},{14,12},{1,9},{3,11}... | collective-permute-start | bytes 196616 | tf_op jit(solution)/shard_map/ppermute | solution.py:98
  3.9 4.3 %collective-permute-start.1 = (f32[16,1024]{1,0:T(8,128)S(1)}, f32[16,1024]{1,0:T(8,128)S(1)}, u32[]{:S(2)}, u32[]{:S(2)}) collective-permute-start(f32[16,1024]{1,0:T(8,128)S(1)} %pad_maximum_fusion), channel_id=1, source_target_pairs={{0,4},{2,6},{4,0},{6,2},{8,12},{10,14},{12,8},{14,10},{1,13},{3,15... | collective-permute-start | bytes 196616 | tf_op jit(solution)/shard_map/ppermute | solution.py:98
  6.1 2.1 %collective-permute-start.2 = (f32[8,1024]{1,0:T(8,128)S(1)}, f32[8,1024]{1,0:T(8,128)S(1)}, u32[]{:S(2)}, u32[]{:S(2)}) collective-permute-start(f32[8,1024]{1,0:T(8,128)S(1)} %slice.5), channel_id=1, source_target_pairs={{0,1},{1,0},{2,3},{3,2},{4,5},{5,4},{6,7},{7,6},{8,9},{9,8},{10,11... | collective-permute-start | bytes 98312 | tf_op jit(solution)/shard_map/ppermute | solution.py:101
  11.8 3.9 %collective-permute-start.3 = (f32[8,1024]{1,0:T(8,128)S(1)}, f32[8,1024]{1,0:T(8,128)S(1)}, u32[]{:S(2)}, u32[]{:S(2)}) collective-permute-start(f32[8,1024]{1,0:T(8,128)S(1)} %get-tuple-element.20), channel_id=1, source_target_pairs={{0,2},{2,0},{4,6},{6,4},{8,10},{10,8},{12,14},{14,12},{1,3},{3,1},... | collective-permute-start | bytes 98312 | tf_op jit(solution)/shard_map/ppermute | solution.py:98
  15.7 1.6 %collective-permute-start.4 = (f32[8,1024]{1,0:T(8,128)S(1)}, f32[8,1024]{1,0:T(8,128)S(1)}, u32[]{:S(2)}, u32[]{:S(2)}) collective-permute-start(f32[8,1024]{1,0:T(8,128)S(1)} %add.9), channel_id=1, source_target_pairs={{0,1},{1,0},{2,3},{3,2},{4,5},{5,4},{6,7},{7,6},{8,9},{9,8},{10,11... | collective-permute-start | bytes 98312 | tf_op jit(solution)/shard_map/ppermute | solution.py:101

commit v5 on v4

--- a/solution.py
+++ b/solution.py
@@ -24,11 +24,13 @@
 
 
 def factors(points, left):
-    norms = jnp.sum(points * points, axis=0, keepdims=True)
     high, middle, low = three_parts(-2.0 * points if left else points)
-    ones = [jnp.ones_like(norms)] * 3
-    rows = [*three_parts(norms), *ones] if left else [*ones, *three_parts(norms)]
-    rows.append(jnp.zeros((DEPTH - 54, points.shape[1]), jnp.float32))
+    kept = -0.5 * high if left else high
+    norms = [jnp.sum(kept * kept, axis=0, keepdims=True), jnp.sum((points - kept) * (points + kept), axis=0, keepdims=True)]
+    norms = [part for norm in norms for part in three_parts(norm)]
+    ones = [jnp.ones_like(norms[0])] * len(norms)
+    rows = norms + ones if left else ones + norms
+    rows.append(jnp.zeros((DEPTH - 60, points.shape[1]), jnp.float32))
     order = [high, high, middle, high, low, middle] if left else [high, middle, high, low, high, middle]
     return jnp.concatenate(order + rows, axis=0)
 

time: 18.1 us -> 18.2 us (level)
  no operation moved by 1% of the time
where the time goes in v5:
time: 18.2 us; the launch traced here: 18 us
  Pallas kernels  7.51 us (41%)
  starting transfers between devices  7.4 us (41%)
  waiting for transfers between devices  1.6 us (9%)
  other arithmetic  1.48 us (8%)
    pallas_call x3, Pallas kernels, tiles(): pl.pallas_call(lambda *refs: tile_kernel(known, made, *refs), out_shape=[...  7.51 us
    ppermute x3, starting transfers between devices, fetch(): return lax.ppermute(array, ('blk', 'section'), pairs)  6.61 us
    ppermute x2, waiting for transfers between devices, swap(): return lax.ppermute(array, 'section', [(0, 1), (1, 0)])  0.87 us
    div x1, other arithmetic, local(): mine = jnp.concatenate([points / scales[:, None], rhs], axis=0)  0.84 us
    ppermute x2, starting transfers between devices, swap(): return lax.ppermute(array, 'section', [(0, 1), (1, 0)])  0.78 us
    ppermute x3, waiting for transfers between devices, fetch(): return lax.ppermute(array, ('blk', 'section'), pairs)  0.73 us
    add x1, other arithmetic, local(): return total + swap(total) + NOISE * rhs  0.62 us
  transfers between devices with their start and end apart: 5, of which 3 were waited for; matrix products, arithmetic and copies ran while one was open for 0% of the time, Pallas kernels for 22%

profile of v5, /device:TPU:0, one launch (start us, length us, event | category | flops | bytes accessed | tf_op | source)
XLA Modules:
  0.0 18.0 jit_solution(14244129965624054836)
XLA Ops:
  0.0 0.0 copy-start
  0.0 0.8 %broadcast_divide_fusion.refs_0_ = f32[8,1024]{1,0:T(8,128)S(1)} fusion(f32[8,1024]{1,0:T(8,128)} %param.3, f32[8]{0:T(128)} %param.5), kind=kLoop, calls=%fused_computation.2 | loop fusion | flops 8192 | bytes 65568 | tf_op jit(solution)/shard_map/div | solution.py:96
  0.8 0.0 copy-done
  0.9 3.0 %collective-permute-start = (f32[16,1024]{1,0:T(8,128)S(1)}, f32[16,1024]{1,0:T(8,128)S(1)}, u32[]{:S(2)}, u32[]{:S(2)}) collective-permute-start(f32[16,1024]{1,0:T(8,128)S(1)} %pad_maximum_fusion), channel_id=1, source_target_pairs={{0,2},{2,0},{4,6},{6,4},{8,10},{10,8},{12,14},{14,12},{1,9},{3,11}... | collective-permute-start | bytes 196616 | tf_op jit(solution)/shard_map/ppermute | solution.py:100
  3.9 1.6 %collective-permute-start.1 = (f32[16,1024]{1,0:T(8,128)S(1)}, f32[16,1024]{1,0:T(8,128)S(1)}, u32[]{:S(2)}, u32[]{:S(2)}) collective-permute-start(f32[16,1024]{1,0:T(8,128)S(1)} %pad_maximum_fusion), channel_id=1, source_target_pairs={{0,4},{2,6},{4,0},{6,2},{8,12},{10,14},{12,8},{14,10},{1,13},{3,15... | collective-permute-start | bytes 196616 | tf_op jit(solution)/shard_map/ppermute | solution.py:100
  5.5 0.7 %collective-permute-done.refs_1_ = f32[16,1024]{1,0:T(8,128)S(1)} collective-permute-done((f32[16,1024]{1,0:T(8,128)S(1)}, f32[16,1024]{1,0:T(8,128)S(1)}, u32[]{:S(2)}, u32[]{:S(2)}) %collective-permute-start) | collective-permute-done | bytes 65568 | tf_op jit(solution)/shard_map/ppermute | solution.py:100
  6.1 0.0 collective-permute-start.2
  6.2 2.0 %shard_map.37 = (f32[8,1024]{1,0:T(8,128)S(1)}, bf16[1024,64]{1,0:T(8,128)(2,1)S(1)}, bf16[64,1024]{1,0:T(8,128)(2,1)S(1)}) custom-call(f32[8,1024]{1,0:T(8,128)S(1)} %broadcast_divide_fusion.refs_0_, f32[16,1024]{1,0:T(8,128)S(1)} %collective-permute-done.refs_1_, f32[8,1024]{1,0:T(8,128)S(1)} %broadcast_in_dim.4.refs_2_.refs_4_), custom_call_target="tpu_custom_call" | custom-call | flops 167772160 | bytes 131072 | tf_op jit(solution)/shard_map/pallas_call | solution.py:80
  8.2 0.0 collective-permute-done.1.refs_2_.refs_1_
  8.2 0.0 collective-permute-done.2
  8.2 3.6 %shard_map.38 = (f32[8,1024]{1,0:T(8,128)S(1)}, bf16[1024,64]{1,0:T(8,128)(2,1)S(1)}, bf16[64,1024]{1,0:T(8,128)(2,1)}) custom-call(f32[8,1024]{1,0:T(8,128)S(1)} %broadcast_select_fusion.refs_0_, f32[16,1024]{1,0:T(8,128)S(1)} %collective-permute-done.refs_1_, f32[16,1024]{1,0:T(8,128)S(1)} %collective-permute-done.1.refs_2_.refs_1_, ...), custom_call_target="tpu_custom_call" | custom-call | flops 335544320 | bytes 131072 | tf_op jit(solution)/shard_map/pallas_call | solution.py:80
  11.9 2.0 %collective-permute-start.3 = (f32[8,1024]{1,0:T(8,128)S(1)}, f32[8,1024]{1,0:T(8,128)S(1)}, u32[]{:S(2)}, u32[]{:S(2)}) collective-permute-start(f32[8,1024]{1,0:T(8,128)S(1)} %get-tuple-element.20), channel_id=1, source_target_pairs={{0,2},{2,0},{4,6},{6,4},{8,10},{10,8},{12,14},{14,12},{1,3},{3,1},... | collective-permute-start | bytes 98312 | tf_op jit(solution)/shard_map/ppermute | solution.py:100
  13.9 1.9 %shard_map.39 = f32[8,1024]{1,0:T(8,128)S(1)} custom-call(bf16[64,1024]{1,0:T(8,128)(2,1)S(1)} %get-tuple-element.13.refs_0_, f32[16,1024]{1,0:T(8,128)S(1)} %collective-permute-done.1.refs_2_.refs_1_, bf16[1024,64]{1,0:T(8,128)(2,1)S(1)} %get-tuple-element.18.refs_2_, f32[8,1024]{1,0:T(8,128)S(1)} %get-tuple-element.19.refs_3_), custom_call_target="tpu_custom_call" | custom-call | flops 167772160 | bytes 131072 | tf_op jit(solution)/shard_map/pallas_call | solution.py:80
  15.7 0.1 collective-permute-done.3
  15.8 0.8 %collective-permute-start.4 = (f32[8,1024]{1,0:T(8,128)S(1)}, f32[8,1024]{1,0:T(8,128)S(1)}, u32[]{:S(2)}, u32[]{:S(2)}) collective-permute-start(f32[8,1024]{1,0:T(8,128)S(1)} %add.9), channel_id=1, source_target_pairs={{0,1},{1,0},{2,3},{3,2},{4,5},{5,4},{6,7},{7,6},{8,9},{9,8},{10,11... | collective-permute-start | bytes 98312 | tf_op jit(solution)/shard_map/ppermute | solution.py:103
  16.5 0.9 %collective-permute-done.4 = f32[8,1024]{1,0:T(8,128)S(1)} collective-permute-done((f32[8,1024]{1,0:T(8,128)S(1)}, f32[8,1024]{1,0:T(8,128)S(1)}, u32[]{:S(2)}, u32[]{:S(2)}) %collective-permute-start.4) | collective-permute-done | bytes 32800 | tf_op jit(solution)/shard_map/ppermute | solution.py:103
  17.4 0.6 %multiply_add_fusion = f32[8,1024]{1,0:T(8,128)} fusion(f32[8,1024]{1,0:T(8,128)S(1)} %copy-done, f32[8,1024]{1,0:T(8,128)S(1)} %add.9, f32[8,1024]{1,0:T(8,128)S(1)} %collective-permute-done.4), kind=kLoop, calls=%fused_computation.1 | loop fusion | flops 24576 | bytes 131072 | tf_op jit(solution)/shard_map/add | solution.py:118
  (5 shorter events, 0.0 us)
Async XLA Ops:
  0.0 0.8 %copy-start = (f32[8,1024]{1,0:T(8,128)S(1)}, f32[8,1024]{1,0:T(8,128)}, u32[]{:S(2)}) copy-start(f32[8,1024]{1,0:T(8,128)} %param.4) | copy-start | bytes 98308
  0.9 5.3 %collective-permute-start = (f32[16,1024]{1,0:T(8,128)S(1)}, f32[16,1024]{1,0:T(8,128)S(1)}, u32[]{:S(2)}, u32[]{:S(2)}) collective-permute-start(f32[16,1024]{1,0:T(8,128)S(1)} %pad_maximum_fusion), channel_id=1, source_target_pairs={{0,2},{2,0},{4,6},{6,4},{8,10},{10,8},{12,14},{14,12},{1,9},{3,11}... | collective-permute-start | bytes 196616 | tf_op jit(solution)/shard_map/ppermute | solution.py:100
  3.9 4.3 %collective-permute-start.1 = (f32[16,1024]{1,0:T(8,128)S(1)}, f32[16,1024]{1,0:T(8,128)S(1)}, u32[]{:S(2)}, u32[]{:S(2)}) collective-permute-start(f32[16,1024]{1,0:T(8,128)S(1)} %pad_maximum_fusion), channel_id=1, source_target_pairs={{0,4},{2,6},{4,0},{6,2},{8,12},{10,14},{12,8},{14,10},{1,13},{3,15... | collective-permute-start | bytes 196616 | tf_op jit(solution)/shard_map/ppermute | solution.py:100
  6.1 2.1 %collective-permute-start.2 = (f32[8,1024]{1,0:T(8,128)S(1)}, f32[8,1024]{1,0:T(8,128)S(1)}, u32[]{:S(2)}, u32[]{:S(2)}) collective-permute-start(f32[8,1024]{1,0:T(8,128)S(1)} %slice.5), channel_id=1, source_target_pairs={{0,1},{1,0},{2,3},{3,2},{4,5},{5,4},{6,7},{7,6},{8,9},{9,8},{10,11... | collective-permute-start | bytes 98312 | tf_op jit(solution)/shard_map/ppermute | solution.py:103
  11.9 3.9 %collective-permute-start.3 = (f32[8,1024]{1,0:T(8,128)S(1)}, f32[8,1024]{1,0:T(8,128)S(1)}, u32[]{:S(2)}, u32[]{:S(2)}) collective-permute-start(f32[8,1024]{1,0:T(8,128)S(1)} %get-tuple-element.20), channel_id=1, source_target_pairs={{0,2},{2,0},{4,6},{6,4},{8,10},{10,8},{12,14},{14,12},{1,3},{3,1},... | collective-permute-start | bytes 98312 | tf_op jit(solution)/shard_map/ppermute | solution.py:100
  15.8 1.6 %collective-permute-start.4 = (f32[8,1024]{1,0:T(8,128)S(1)}, f32[8,1024]{1,0:T(8,128)S(1)}, u32[]{:S(2)}, u32[]{:S(2)}) collective-permute-start(f32[8,1024]{1,0:T(8,128)S(1)} %add.9), channel_id=1, source_target_pairs={{0,1},{1,0},{2,3},{3,2},{4,5},{5,4},{6,7},{7,6},{8,9},{9,8},{10,11... | collective-permute-start | bytes 98312 | tf_op jit(solution)/shard_map/ppermute | solution.py:103

commit v6 on v5

--- a/solution.py
+++ b/solution.py
@@ -58,8 +58,8 @@
         high = values.astype(jnp.bfloat16).astype(jnp.float32)
         both = jnp.concatenate([high, values - high], axis=0).astype(jnp.bfloat16)
         single = jnp.concatenate([high, jnp.zeros_like(high)], axis=0).astype(jnp.bfloat16)
-        for j in range(0, column.shape[1], STEP):
-            for i in range(0, right_ref.shape[1], STEP):
+        for i in range(0, right_ref.shape[1], STEP):
+            for j in range(0, column.shape[1], STEP):
                 product = multiply(left_ref[j : j + STEP], right_ref[:, i : i + STEP])
                 squared = jnp.maximum(product, 1e-30)
                 scaled = squared * lax.rsqrt(squared)

time: 18.2 us -> 18.2 us (level)
  no operation moved by 1% of the time
where the time goes in v6:
time: 18.2 us; the launch traced here: 18 us
  Pallas kernels  7.55 us (41%)
  starting transfers between devices  7.38 us (41%)
  waiting for transfers between devices  1.59 us (9%)
  other arithmetic  1.48 us (8%)
    pallas_call x3, Pallas kernels, tiles(): pl.pallas_call(lambda *refs: tile_kernel(known, made, *refs), out_shape=[...  7.55 us
    ppermute x3, starting transfers between devices, fetch(): return lax.ppermute(array, ('blk', 'section'), pairs)  6.62 us
    ppermute x2, waiting for transfers between devices, swap(): return lax.ppermute(array, 'section', [(0, 1), (1, 0)])  0.87 us
    div x1, other arithmetic, local(): mine = jnp.concatenate([points / scales[:, None], rhs], axis=0)  0.84 us
    ppermute x2, starting transfers between devices, swap(): return lax.ppermute(array, 'section', [(0, 1), (1, 0)])  0.76 us
    ppermute x3, waiting for transfers between devices, fetch(): return lax.ppermute(array, ('blk', 'section'), pairs)  0.72 us
    add x1, other arithmetic, local(): return total + swap(total) + NOISE * rhs  0.62 us
  transfers between devices with their start and end apart: 5, of which 3 were waited for; matrix products, arithmetic and copies ran while one was open for 0% of the time, Pallas kernels for 22%

profile of v6, /device:TPU:0, one launch (start us, length us, event | category | flops | bytes accessed | tf_op | source)
XLA Modules:
  0.0 18.0 jit_solution(15788053985028843320)
XLA Ops:
  0.0 0.0 copy-start
  0.0 0.8 %broadcast_divide_fusion.refs_0_ = f32[8,1024]{1,0:T(8,128)S(1)} fusion(f32[8,1024]{1,0:T(8,128)} %param.3, f32[8]{0:T(128)} %param.5), kind=kLoop, calls=%fused_computation.2 | loop fusion | flops 8192 | bytes 65568 | tf_op jit(solution)/shard_map/div | solution.py:96
  0.8 0.0 copy-done
  0.9 3.0 %collective-permute-start = (f32[16,1024]{1,0:T(8,128)S(1)}, f32[16,1024]{1,0:T(8,128)S(1)}, u32[]{:S(2)}, u32[]{:S(2)}) collective-permute-start(f32[16,1024]{1,0:T(8,128)S(1)} %pad_maximum_fusion), channel_id=1, source_target_pairs={{0,2},{2,0},{4,6},{6,4},{8,10},{10,8},{12,14},{14,12},{1,9},{3,11}... | collective-permute-start | bytes 196616 | tf_op jit(solution)/shard_map/ppermute | solution.py:100
  3.9 1.6 %collective-permute-start.1 = (f32[16,1024]{1,0:T(8,128)S(1)}, f32[16,1024]{1,0:T(8,128)S(1)}, u32[]{:S(2)}, u32[]{:S(2)}) collective-permute-start(f32[16,1024]{1,0:T(8,128)S(1)} %pad_maximum_fusion), channel_id=1, source_target_pairs={{0,4},{2,6},{4,0},{6,2},{8,12},{10,14},{12,8},{14,10},{1,13},{3,15... | collective-permute-start | bytes 196616 | tf_op jit(solution)/shard_map/ppermute | solution.py:100
  5.5 0.7 %collective-permute-done.refs_1_ = f32[16,1024]{1,0:T(8,128)S(1)} collective-permute-done((f32[16,1024]{1,0:T(8,128)S(1)}, f32[16,1024]{1,0:T(8,128)S(1)}, u32[]{:S(2)}, u32[]{:S(2)}) %collective-permute-start) | collective-permute-done | bytes 65568 | tf_op jit(solution)/shard_map/ppermute | solution.py:100
  6.1 0.0 collective-permute-start.2
  6.2 2.0 %shard_map.37 = (f32[8,1024]{1,0:T(8,128)S(1)}, bf16[1024,64]{1,0:T(8,128)(2,1)S(1)}, bf16[64,1024]{1,0:T(8,128)(2,1)S(1)}) custom-call(f32[8,1024]{1,0:T(8,128)S(1)} %broadcast_divide_fusion.refs_0_, f32[16,1024]{1,0:T(8,128)S(1)} %collective-permute-done.refs_1_, f32[8,1024]{1,0:T(8,128)S(1)} %broadcast_in_dim.4.refs_2_.refs_4_), custom_call_target="tpu_custom_call" | custom-call | flops 167772160 | bytes 131072 | tf_op jit(solution)/shard_map/pallas_call | solution.py:80
  8.2 0.0 collective-permute-done.1.refs_2_.refs_1_
  8.2 0.0 collective-permute-done.2
  8.3 3.6 %shard_map.38 = (f32[8,1024]{1,0:T(8,128)S(1)}, bf16[1024,64]{1,0:T(8,128)(2,1)S(1)}, bf16[64,1024]{1,0:T(8,128)(2,1)}) custom-call(f32[8,1024]{1,0:T(8,128)S(1)} %broadcast_select_fusion.refs_0_, f32[16,1024]{1,0:T(8,128)S(1)} %collective-permute-done.refs_1_, f32[16,1024]{1,0:T(8,128)S(1)} %collective-permute-done.1.refs_2_.refs_1_, ...), custom_call_target="tpu_custom_call" | custom-call | flops 335544320 | bytes 131072 | tf_op jit(solution)/shard_map/pallas_call | solution.py:80
  11.9 2.0 %collective-permute-start.3 = (f32[8,1024]{1,0:T(8,128)S(1)}, f32[8,1024]{1,0:T(8,128)S(1)}, u32[]{:S(2)}, u32[]{:S(2)}) collective-permute-start(f32[8,1024]{1,0:T(8,128)S(1)} %get-tuple-element.20), channel_id=1, source_target_pairs={{0,2},{2,0},{4,6},{6,4},{8,10},{10,8},{12,14},{14,12},{1,3},{3,1},... | collective-permute-start | bytes 98312 | tf_op jit(solution)/shard_map/ppermute | solution.py:100
  13.9 1.9 %shard_map.39 = f32[8,1024]{1,0:T(8,128)S(1)} custom-call(bf16[64,1024]{1,0:T(8,128)(2,1)S(1)} %get-tuple-element.13.refs_0_, f32[16,1024]{1,0:T(8,128)S(1)} %collective-permute-done.1.refs_2_.refs_1_, bf16[1024,64]{1,0:T(8,128)(2,1)S(1)} %get-tuple-element.18.refs_2_, f32[8,1024]{1,0:T(8,128)S(1)} %get-tuple-element.19.refs_3_), custom_call_target="tpu_custom_call" | custom-call | flops 167772160 | bytes 131072 | tf_op jit(solution)/shard_map/pallas_call | solution.py:80
  15.8 0.1 collective-permute-done.3
  15.8 0.7 %collective-permute-start.4 = (f32[8,1024]{1,0:T(8,128)S(1)}, f32[8,1024]{1,0:T(8,128)S(1)}, u32[]{:S(2)}, u32[]{:S(2)}) collective-permute-start(f32[8,1024]{1,0:T(8,128)S(1)} %add.9), channel_id=1, source_target_pairs={{0,1},{1,0},{2,3},{3,2},{4,5},{5,4},{6,7},{7,6},{8,9},{9,8},{10,11... | collective-permute-start | bytes 98312 | tf_op jit(solution)/shard_map/ppermute | solution.py:103
  16.6 0.9 %collective-permute-done.4 = f32[8,1024]{1,0:T(8,128)S(1)} collective-permute-done((f32[8,1024]{1,0:T(8,128)S(1)}, f32[8,1024]{1,0:T(8,128)S(1)}, u32[]{:S(2)}, u32[]{:S(2)}) %collective-permute-start.4) | collective-permute-done | bytes 32800 | tf_op jit(solution)/shard_map/ppermute | solution.py:103
  17.4 0.6 %multiply_add_fusion = f32[8,1024]{1,0:T(8,128)} fusion(f32[8,1024]{1,0:T(8,128)S(1)} %copy-done, f32[8,1024]{1,0:T(8,128)S(1)} %add.9, f32[8,1024]{1,0:T(8,128)S(1)} %collective-permute-done.4), kind=kLoop, calls=%fused_computation.1 | loop fusion | flops 24576 | bytes 131072 | tf_op jit(solution)/shard_map/add | solution.py:118
  (5 shorter events, 0.0 us)
Async XLA Ops:
  0.0 0.8 %copy-start = (f32[8,1024]{1,0:T(8,128)S(1)}, f32[8,1024]{1,0:T(8,128)}, u32[]{:S(2)}) copy-start(f32[8,1024]{1,0:T(8,128)} %param.4) | copy-start | bytes 98308
  0.9 5.3 %collective-permute-start = (f32[16,1024]{1,0:T(8,128)S(1)}, f32[16,1024]{1,0:T(8,128)S(1)}, u32[]{:S(2)}, u32[]{:S(2)}) collective-permute-start(f32[16,1024]{1,0:T(8,128)S(1)} %pad_maximum_fusion), channel_id=1, source_target_pairs={{0,2},{2,0},{4,6},{6,4},{8,10},{10,8},{12,14},{14,12},{1,9},{3,11}... | collective-permute-start | bytes 196616 | tf_op jit(solution)/shard_map/ppermute | solution.py:100
  3.9 4.3 %collective-permute-start.1 = (f32[16,1024]{1,0:T(8,128)S(1)}, f32[16,1024]{1,0:T(8,128)S(1)}, u32[]{:S(2)}, u32[]{:S(2)}) collective-permute-start(f32[16,1024]{1,0:T(8,128)S(1)} %pad_maximum_fusion), channel_id=1, source_target_pairs={{0,4},{2,6},{4,0},{6,2},{8,12},{10,14},{12,8},{14,10},{1,13},{3,15... | collective-permute-start | bytes 196616 | tf_op jit(solution)/shard_map/ppermute | solution.py:100
  6.1 2.1 %collective-permute-start.2 = (f32[8,1024]{1,0:T(8,128)S(1)}, f32[8,1024]{1,0:T(8,128)S(1)}, u32[]{:S(2)}, u32[]{:S(2)}) collective-permute-start(f32[8,1024]{1,0:T(8,128)S(1)} %slice.5), channel_id=1, source_target_pairs={{0,1},{1,0},{2,3},{3,2},{4,5},{5,4},{6,7},{7,6},{8,9},{9,8},{10,11... | collective-permute-start | bytes 98312 | tf_op jit(solution)/shard_map/ppermute | solution.py:103
  11.9 3.9 %collective-permute-start.3 = (f32[8,1024]{1,0:T(8,128)S(1)}, f32[8,1024]{1,0:T(8,128)S(1)}, u32[]{:S(2)}, u32[]{:S(2)}) collective-permute-start(f32[8,1024]{1,0:T(8,128)S(1)} %get-tuple-element.20), channel_id=1, source_target_pairs={{0,2},{2,0},{4,6},{6,4},{8,10},{10,8},{12,14},{14,12},{1,3},{3,1},... | collective-permute-start | bytes 98312 | tf_op jit(solution)/shard_map/ppermute | solution.py:100
  15.8 1.6 %collective-permute-start.4 = (f32[8,1024]{1,0:T(8,128)S(1)}, f32[8,1024]{1,0:T(8,128)S(1)}, u32[]{:S(2)}, u32[]{:S(2)}) collective-permute-start(f32[8,1024]{1,0:T(8,128)S(1)} %add.9), channel_id=1, source_target_pairs={{0,1},{1,0},{2,3},{3,2},{4,5},{5,4},{6,7},{7,6},{8,9},{9,8},{10,11... | collective-permute-start | bytes 98312 | tf_op jit(solution)/shard_map/ppermute | solution.py:103
